TPU v7x, 32 devices: a whole 2x2x4 slice. The times are simulated.
32 devices in a mesh: chan: 8 (over z, y), tm: 4 (over x, core).
Axes of the slice: x: 2, y: 2, z: 4, core: 2. Of those that a mesh axis runs over, the one named last changes fastest.
Arguments:
- visibilities: bfloat16 [16, 16, 2, 512, 512], P('chan', 'tm'), may hold values from -640 to 640, as said below
- model: bfloat16 [16, 16, 2, 512, 512], P('chan', 'tm'), may hold values from -32 to 32, as said below
- beam_left: bfloat16 [8, 256, 128], replicated, may hold values from -0.5 to 0.5
- beam_right: bfloat16 [8, 256, 128], replicated, may hold values from -0.0234375 to 0.0234375
- weight_index: int32 [16, 16], P('chan'), may hold values from 0 to 7
- target_bank: int32 [16, 16, 16], P('chan', 'tm'), may hold values from 0 to 7
- widths: int32 [16], P('chan'), may hold values from 0 to 2, as said below
Outputs:
- covariance: float32 [4096, 256], P('chan')
Inputs may be any that keep to these rules, and one draw needn't show every extreme that they name: `visibilities`: real part at index 0 and imaginary part at index 1; each matrix is Hermitian in its last two dimensions. `model`: real part at index 0 and imaginary part at index 1; each matrix is Hermitian in its last two dimensions. `widths`: some channel has width 2.
All inputs are finite; a program needn't handle non-finite values.
Results may differ from a plain program's by a relative error of at most 0.0041.
Values sent between devices are 32-bit elements; how exact they have to be, the bound alone decides.
No kernel may reach another device: no remote copies, remote signals or barrier semaphores. Data moves between devices by JAX's collectives and lax.ppermute only.
A program may use at most 256 MiB of HBM per device.

v0:
```python
import jax
import jax.numpy as jnp
from jax import lax
from jax.sharding import PartitionSpec as P

N = 512
BLK = 128
BEAMS = 256
BANKS = 8
ITERS = 6
HW = 2


epsilon = 1e-06


def extended_2(cells, sides, width):
    for axis, dim in sides:
        count = lax.axis_size(axis)
        ends = count - 1
        head = lax.slice_in_dim(cells, 0, width, axis=dim)
        tail = lax.slice_in_dim(cells, cells.shape[dim] - width, cells.shape[dim], axis=dim)
        cells = jnp.concatenate(
            [
                lax.ppermute(tail, axis, [(i, (i + 1) % count) for i in range(ends)]),
                cells,
                lax.ppermute(head, axis, [((i + 1) % count, i) for i in range(ends)]),
            ],
            axis=dim,
        )
    return cells


def contract_rows(vectors, matrix):
    return jnp.einsum("...kq,...qp->...kp", vectors, matrix, precision=lax.Precision.HIGHEST)


def stefcal(visibilities, model):
    vis_re = visibilities[..., 0, :, :].astype(jnp.float32)
    vis_im = visibilities[..., 1, :, :].astype(jnp.float32)
    mod_re = model[..., 0, :, :].astype(jnp.float32)
    mod_im = model[..., 1, :, :].astype(jnp.float32)
    cross_re = mod_re * vis_re + mod_im * vis_im
    cross_im = mod_im * vis_re - mod_re * vis_im
    power = mod_re * mod_re + mod_im * mod_im
    gain_re = jnp.ones(vis_re.shape[:-1], jnp.float32)
    gain_im = jnp.zeros(vis_re.shape[:-1], jnp.float32)
    for sweep_index in range(ITERS):
        paired = jnp.stack([gain_re, gain_im], axis=-2)
        with_real = contract_rows(paired, cross_re)
        with_imag = contract_rows(paired, cross_im)
        magnitude = (gain_re * gain_re + gain_im * gain_im)[..., None, :]
        denominator = contract_rows(magnitude, power)[..., 0, :] + epsilon
        num_re = with_real[..., 0, :] - with_imag[..., 1, :]
        num_im = with_imag[..., 0, :] + with_real[..., 1, :]
        new_re = num_re / denominator
        new_im = num_im / denominator
        if sweep_index % 2 == 1:
            gain_re = 0.5 * (new_re + gain_re)
            gain_im = 0.5 * (new_im + gain_im)
        else:
            gain_re = new_re
            gain_im = new_im
    return (gain_re, gain_im)


def align_phase(gain_re, gain_im):
    first_re = gain_re[..., :1]
    first_im = gain_im[..., :1]
    divisor = jnp.maximum(jnp.sqrt(first_re * first_re + first_im * first_im), 1.0)
    unit_re = first_re / divisor
    unit_im = -first_im / divisor
    return (gain_re * unit_re - gain_im * unit_im, gain_re * unit_im + gain_im * unit_re)


def calibrate(smooth_re, smooth_im, visibilities):
    vis_re = visibilities[..., 0, :, :].astype(jnp.float32)
    vis_im = visibilities[..., 1, :, :].astype(jnp.float32)
    denominator = jnp.maximum(smooth_re * smooth_re + smooth_im * smooth_im, 1.0)
    inv_re = smooth_re / denominator
    inv_im = -smooth_im / denominator
    row_re = inv_re[..., :, None]
    row_im = inv_im[..., :, None]
    col_re = inv_re[..., None, :]
    col_im = inv_im[..., None, :]
    left_re = row_re * vis_re - row_im * vis_im
    left_im = row_re * vis_im + row_im * vis_re
    out_re = left_re * col_re + left_im * col_im
    out_im = left_im * col_re - left_re * col_im
    return jnp.stack([out_re, out_im], axis=-3).astype(jnp.bfloat16)


def local(visibilities, model, beam_left, beam_right, weight_index, target_bank, widths):
    local_channels = visibilities.shape[0]
    local_intervals = visibilities.shape[1]
    group_count = N // BLK
    gain_re, gain_im = stefcal(visibilities, model)
    ref_re, ref_im = align_phase(gain_re, gain_im)
    stacked = jnp.stack([ref_re, ref_im], axis=2)
    extended = extended_2(stacked, (("tm", 1),), HW)
    interval = lax.axis_index("tm") * local_intervals + jnp.arange(local_intervals, dtype=jnp.int32)
    all_intervals = lax.axis_size("tm") * local_intervals
    summed = jnp.zeros_like(stacked)
    counts = jnp.zeros((local_channels, local_intervals), jnp.float32)
    for offset in range(-HW, HW + 1):
        inside = (
            (abs(offset) <= widths[:, None])
            & (interval[None, :] + offset >= 0)
            & (interval[None, :] + offset < all_intervals)
        ).astype(jnp.float32)
        summed = (
            summed
            + inside[:, :, None, None] * extended[:, HW + offset : HW + offset + local_intervals]
        )
        counts = counts + inside
    smooth = summed / counts[:, :, None, None]
    calibrated = calibrate(smooth[:, :, 0], smooth[:, :, 1], visibilities)
    pieces = calibrated.reshape(
        (local_channels, local_intervals, 2, group_count, BLK, group_count, BLK)
    )
    left_groups = beam_left[weight_index].reshape(
        (local_channels, group_count, group_count, BEAMS, BLK)
    )
    right_groups = beam_right[weight_index].reshape(
        (local_channels, group_count, group_count, BEAMS, BLK)
    )
    bank_hits = (target_bank[..., None] == jnp.arange(BANKS, dtype=jnp.int32)).astype(jnp.float32)
    bank_hits = bank_hits.reshape(
        (local_channels, local_intervals, group_count, group_count, BANKS)
    )

    def per_channel(accumulated, channel_data):
        piece_one, left_one, right_one, hits_one = channel_data
        formed = jnp.einsum(
            "ijux,tsixjy->tijsuy", left_one, piece_one, preferred_element_type=jnp.float32
        ).astype(jnp.bfloat16)
        contrib = jnp.einsum(
            "tijsuy,ijvy->tijsuv", formed, right_one, preferred_element_type=jnp.float32
        )
        accumulated = accumulated + jnp.einsum(
            "tijk,tijsuv->ksuv", hits_one, contrib, precision=lax.Precision.HIGHEST
        )
        return (accumulated, None)

    start_banks = jnp.zeros((BANKS, 2, BEAMS, BEAMS), jnp.float32)
    bank_terms, unused = lax.scan(
        per_channel, start_banks, (pieces, left_groups, right_groups, bank_hits)
    )
    bank_terms = bank_terms.reshape((BANKS * 2 * BEAMS, BEAMS))
    shares = lax.psum_scatter(bank_terms, "chan", scatter_dimension=0, tiled=True)
    result = lax.psum(shares, "tm")
    return result


def solution(mesh):
    return jax.shard_map(
        local,
        mesh=mesh,
        in_specs=(
            P("chan", "tm", None, None, None),
            P("chan", "tm", None, None, None),
            P(),
            P(),
            P("chan", None),
            P("chan", "tm", None),
            P("chan"),
        ),
        out_specs=P("chan", None),
        check_vma=False,
    )
```

profile of v0, /device:TPU:0, one launch (start us, length us, event | category | flops | bytes accessed | tf_op | source)
XLA Modules:
  0.0 508.5 jit_solution(5910599854224777322)
XLA Ops:
  6.5 7.7 %fusion.81 = f32[2,4,1,512]{3,2,1,0:T(1,128)S(1)} fusion(bf16[2,4,2,512,512]{4,3,2,1,0:T(8,128)(2,1)} %param.10), kind=kOutput, calls=%fused_computation.151 | convolution fusion | flops 35651584 | bytes 8404992 | tf_op jit(solution)/shard_map/...kq,...qp->...kp/dot_general | solution.py:35
  14.2 7.6 %fusion.20 = (f32[2,4,512,512]{3,2,1,0:T(8,128)S(1)}, f32[2,4,512,512]{3,2,1,0:T(8,128)S(1)}) fusion(bf16[2,4,2,512,512]{4,3,2,1,0:T(8,128)(2,1)} %param.10, bf16[2,4,2,512,512]{4,3,2,1,0:T(8,128)(2,1)} %param.9), kind=kLoop, calls=%fused_computation.30 | loop fusion | flops 20971520 | bytes 33554432 | tf_op jit(solution)/shard_map/add | solution.py:43
  30.1 4.5 fusion.50
  38.7 5.3 %fusion.77 = f32[2,4,1,512]{3,2,1,0:T(1,128)S(1)} fusion(f32[2,4,512,1]{2,1,0,3:T(4,128)S(1)} %get-tuple-element.100, bf16[2,4,2,512,512]{4,3,2,1,0:T(8,128)(2,1)S(1)} %bitcast.243), kind=kOutput, calls=%fused_computation.135 | convolution fusion | flops 35651584 | bytes 8421376 | tf_op jit(solution)/shard_map/...kq,...qp->...kp/dot_general | solution.py:35
  44.0 4.2 fusion.46
  48.2 4.1 fusion.44
  52.4 5.3 %fusion.75 = f32[2,4,1,512]{3,2,1,0:T(1,128)S(1)} fusion(f32[2,4,512,1]{2,1,0,3:T(4,128)S(1)} %get-tuple-element.97, bf16[2,4,2,512,512]{4,3,2,1,0:T(8,128)(2,1)S(1)} %bitcast.243), kind=kOutput, calls=%fused_computation.133 | convolution fusion | flops 35651584 | bytes 8421376 | tf_op jit(solution)/shard_map/...kq,...qp->...kp/dot_general | solution.py:35
  57.7 4.3 fusion.42
  61.9 4.1 fusion.40
  66.1 5.7 %fusion.73 = f32[2,4,1,512]{3,2,1,0:T(1,128)S(1)} fusion(f32[2,4,512,1]{2,1,0,3:T(4,128)S(1)} %get-tuple-element.94, bf16[2,4,2,512,512]{4,3,2,1,0:T(8,128)(2,1)S(1)} %bitcast.243), kind=kOutput, calls=%fused_computation.131 | convolution fusion | flops 35651584 | bytes 8421376 | tf_op jit(solution)/shard_map/...kq,...qp->...kp/dot_general | solution.py:35
  75.9 4.1 fusion.36
  80.0 6.2 %fusion.71 = f32[2,4,1,512]{3,2,1,0:T(1,128)S(1)} fusion(f32[2,4,512,1]{2,1,0,3:T(4,128)S(1)} %get-tuple-element.91, bf16[2,4,2,512,512]{4,3,2,1,0:T(8,128)(2,1)S(1)} %bitcast.243), kind=kOutput, calls=%fused_computation.129 | convolution fusion | flops 35651584 | bytes 8421376 | tf_op jit(solution)/shard_map/...kq,...qp->...kp/dot_general | solution.py:35
  86.2 4.1 fusion.32
  94.5 5.3 %fusion.69 = f32[2,4,1,512]{3,2,1,0:T(1,128)S(1)} fusion(f32[2,4,512,1]{2,1,0,3:T(4,128)S(1)} %get-tuple-element.88, bf16[2,4,2,512,512]{4,3,2,1,0:T(8,128)(2,1)S(1)} %bitcast.243), kind=kOutput, calls=%fused_computation.127 | convolution fusion | flops 35651584 | bytes 8421376 | tf_op jit(solution)/shard_map/...kq,...qp->...kp/dot_general | solution.py:35
  107.8 9.3 %add_convert_fusion = (bf16[2,4,1,512,512]{4,3,2,1,0:T(8,128)(2,1)}, bf16[2,4,1,512,512]{4,3,2,1,0:T(8,128)(2,1)}) fusion(f32[2,4,512]{2,1,0:T(4,128)S(1)} %get-tuple-element.110, f32[2,4,512]{2,1,0:T(4,128)S(1)} %get-tuple-element.109, f32[2,4,512]{2,1,0:T(4,128)S(1)} %get-tuple-element.108, f32[2,4,512]{2,1,0:T(4,128)S(1)} %get-tuple-element.107, ...), kind=kLoop, calls=%fused_computation.37 | loop fusion | flops 33554432 | bytes 16842752 | tf_op jit(solution)/shard_map/convert.3
  117.1 6.9 %stack.45 = bf16[2,4,1,4,128,4,128]{6,5,4,3,1,0,2:T(4,128)(2,1)} reshape(bf16[2,4,1,512,512]{4,3,2,1,0:T(8,128)(2,1)} %get-tuple-element.105) | data formatting | bytes 8388608 | tf_op jit(solution)/shard_map/stack | solution.py:90
  124.0 6.9 %stack.46 = bf16[2,4,1,4,128,4,128]{6,5,4,3,1,0,2:T(4,128)(2,1)} reshape(bf16[2,4,1,512,512]{4,3,2,1,0:T(8,128)(2,1)} %get-tuple-element.106) | data formatting | bytes 8388608 | tf_op jit(solution)/shard_map/stack | solution.py:90
  130.9 8.7 %pad_maximum_fusion = bf16[2,4,2,4,128,4,128]{6,5,4,3,1,0,2:T(4,128)(2,1)} fusion(bf16[2,4,1,4,128,4,128]{6,5,4,3,1,0,2:T(4,128)(2,1)} %stack.46, bf16[2,4,1,4,128,4,128]{6,5,4,3,1,0,2:T(4,128)(2,1)} %stack.45), kind=kLoop, calls=%fused_computation.35 | loop fusion | flops 4194304 | bytes 16777216 | tf_op jit(solution)/shard_map/stack | solution.py:90
  139.6 226.3 %while.11 = (s32[]{:T(128)}, f32[8,2,256,256]{3,0,2,1:T(8,128)}, f32[2,4,4,4,8]{4,1,3,2,0:T(4,128)S(1)}, bf16[2,4,4,256,128]{4,3,2,1,0:T(8,128)(2,1)S(1)}, bf16[...) while((s32[]{:T(128)}, f32[8,2,256,256]{3,0,2,1:T(8,128)}, ...), condition=%wide.region_1.2_spmd.clone, body=%wide.region_0.1_spmd.clone.sunk | while | flops 4032823296 | bytes 165708912 | solution.py:146
  139.8 6.7 %constant_dynamic-slice_fusion.2 = bf16[1,4,2,4,128,4,128]{6,5,4,3,1,0,2:T(4,128)(2,1)} fusion(bf16[2,4,2,4,128,4,128]{6,5,4,3,1,0,2:T(4,128)(2,1)} %get-tuple-element.215, s32[]{:T(128)} %get-tuple-element.203), kind=kLoop, calls=%fused_computation.15.clone.1 | loop fusion | bytes 8388612 | tf_op jit(solution)/shard_map/while/body/jit(dynamic_index_in_dim)/dynamic_slice | solution.py:146
  146.5 7.5 %copy.392 = bf16[1,4,2,4,128,4,128]{4,6,2,1,5,3,0:T(8,128)(2,1)} copy(bf16[1,4,2,4,128,4,128]{6,5,4,3,1,0,2:T(4,128)(2,1)} %constant_dynamic-slice_fusion.2) | data formatting | bytes 8388608 | tf_op jit(solution)/shard_map/while/body/jit(dynamic_index_in_dim)/dynamic_slice | solution.py:146
  154.0 15.9 %convolution_bitcast_fusion.2 = f32[4,4,4,2,256,256]{4,5,3,0,2,1:T(8,128)} fusion(bf16[1,4,2,4,128,4,128]{4,6,2,1,5,3,0:T(8,128)(2,1)} %copy.392, bf16[2,4,4,256,128]{4,3,2,1,0:T(8,128)(2,1)} %get-tuple-element.216, s32[]{:T(128)} %get-tuple-element.203, bf16[2,4,4,256,128]{4,3,2,1,0:T(8,128)(2,1)S(1)} %get-tuple-element.214), kind=kOutput, calls=%fused_computation.2.clone.1 | convolution fusion | flops 3225419776 | bytes 39846912 | tf_op jit(solution)/shard_map/while/body/eval_jaxpr/tijsuy,ijvy->tijsuv/dot_general | solution.py:137
  169.9 39.9 %copy.393 = f32[4,4,4,2,256,256]{5,0,2,1,4,3:T(4,128)} copy(f32[4,4,4,2,256,256]{4,5,3,0,2,1:T(8,128)} %convolution_bitcast_fusion.2) | data formatting | bytes 67108864 | tf_op jit(solution)/shard_map/while/body/eval_jaxpr/tijsuy,ijvy->tijsuv/transpose | solution.py:137
  209.8 42.9 %bitcast_add_fusion.10 = f32[8,2,256,256]{3,0,2,1:T(8,128)} fusion(f32[8,2,256,256]{3,0,2,1:T(8,128)} %get-tuple-element.204, f32[4,4,4,2,256,256]{5,0,2,1,4,3:T(4,128)} %copy.393, pred[]{:T(512)S(6)} %compare.3, f32[2,4,4,4,8]{4,1,3,2,0:T(4,128)S(1)} %get-tuple-element.213, s32[]{:T(128)} %get-tuple-element.203), kind=kOutput, calls=%fused_computation.6.clone.1 | convolution fusion | flops 807403520 | bytes 41975812 | tf_op jit(solution)/shard_map/while/body/eval_jaxpr/tijk,tijsuv->ksuv/dot_general | solution.py:140
  252.7 6.7 %constant_dynamic-slice_fusion.2 = bf16[1,4,2,4,128,4,128]{6,5,4,3,1,0,2:T(4,128)(2,1)} fusion(bf16[2,4,2,4,128,4,128]{6,5,4,3,1,0,2:T(4,128)(2,1)} %get-tuple-element.215, s32[]{:T(128)} %get-tuple-element.203), kind=kLoop, calls=%fused_computation.15.clone.1 | loop fusion | bytes 8388612 | tf_op jit(solution)/shard_map/while/body/jit(dynamic_index_in_dim)/dynamic_slice | solution.py:146
  259.4 7.5 %copy.392 = bf16[1,4,2,4,128,4,128]{4,6,2,1,5,3,0:T(8,128)(2,1)} copy(bf16[1,4,2,4,128,4,128]{6,5,4,3,1,0,2:T(4,128)(2,1)} %constant_dynamic-slice_fusion.2) | data formatting | bytes 8388608 | tf_op jit(solution)/shard_map/while/body/jit(dynamic_index_in_dim)/dynamic_slice | solution.py:146
  266.9 15.9 %convolution_bitcast_fusion.2 = f32[4,4,4,2,256,256]{4,5,3,0,2,1:T(8,128)} fusion(bf16[1,4,2,4,128,4,128]{4,6,2,1,5,3,0:T(8,128)(2,1)} %copy.392, bf16[2,4,4,256,128]{4,3,2,1,0:T(8,128)(2,1)} %get-tuple-element.216, s32[]{:T(128)} %get-tuple-element.203, bf16[2,4,4,256,128]{4,3,2,1,0:T(8,128)(2,1)S(1)} %get-tuple-element.214), kind=kOutput, calls=%fused_computation.2.clone.1 | convolution fusion | flops 3225419776 | bytes 39846912 | tf_op jit(solution)/shard_map/while/body/eval_jaxpr/tijsuy,ijvy->tijsuv/dot_general | solution.py:137
  282.8 39.9 %copy.393 = f32[4,4,4,2,256,256]{5,0,2,1,4,3:T(4,128)} copy(f32[4,4,4,2,256,256]{4,5,3,0,2,1:T(8,128)} %convolution_bitcast_fusion.2) | data formatting | bytes 67108864 | tf_op jit(solution)/shard_map/while/body/eval_jaxpr/tijsuy,ijvy->tijsuv/transpose | solution.py:137
  322.7 43.3 %bitcast_add_fusion.10 = f32[8,2,256,256]{3,0,2,1:T(8,128)} fusion(f32[8,2,256,256]{3,0,2,1:T(8,128)} %get-tuple-element.204, f32[4,4,4,2,256,256]{5,0,2,1,4,3:T(4,128)} %copy.393, pred[]{:T(512)S(6)} %compare.3, f32[2,4,4,4,8]{4,1,3,2,0:T(4,128)S(1)} %get-tuple-element.213, s32[]{:T(128)} %get-tuple-element.203), kind=kOutput, calls=%fused_computation.6.clone.1 | convolution fusion | flops 807403520 | bytes 41975812 | tf_op jit(solution)/shard_map/while/body/eval_jaxpr/tijk,tijsuv->ksuv/dot_general | solution.py:140
  366.0 5.6 %copy.156 = f32[8,2,256,256]{3,2,1,0:T(8,128)} copy(f32[8,2,256,256]{3,0,2,1:T(8,128)} %get-tuple-element.37) | data formatting | bytes 8388608 | tf_op jit(solution)/shard_map/while | solution.py:146
  371.6 92.4 %reduce-scatter.2.cloned.1.call-done = f32[512,256]{1,0:T(8,128)} async-done(((f32[4096,256]{1,0:T(8,128)}), f32[512,256]{1,0:T(8,128)}) %reduce-scatter.2.cloned.1.call-update) | async-done | bytes 524304 | tf_op jit(solution)/shard_map/reduce_scatter | solution.py:150
  464.0 35.4 %all-reduce.2.cloned.1.call-done = f32[512,256]{1,0:T(8,128)} async-done(((f32[512,256]{1,0:T(8,128)}), f32[512,256]{1,0:T(8,128)}) %all-reduce.2.cloned.1.call-update) | async-done | bytes 524304 | tf_op jit(solution)/shard_map/psum | solution.py:151
  (82 shorter events, 30.7 us)
Async XLA Ops:
  6.5 97.7 %copy-start = (bf16[8,256,128]{2,1,0:T(8,128)(2,1)S(1)}, bf16[8,256,128]{2,1,0:T(8,128)(2,1)}, u32[]{:S(2)}) copy-start(bf16[8,256,128]{2,1,0:T(8,128)(2,1)} %param.12) | copy-start | bytes 1572868
  6.5 457.4 %reduce-scatter.2.cloned.1.call-start = ((), (), s32[]{:S(2)}) async-start(), calls=%async_computation.1 | async-start | bytes 4718592 | tf_op jit(solution)/shard_map/reduce_scatter | solution.py:150
  14.2 7.6 %copy-start.3 = (f32[2,4,2,512]{3,2,1,0:T(2,128)S(1)}, f32[2,4,2,512]{3,2,1,0:T(2,128)}, u32[]{:S(2)}) copy-start(f32[2,4,2,512]{3,2,1,0:T(2,128)} %constant.27.clone.1) | copy-start | bytes 98308
  30.1 8.6 %slice-start = ((s8[8388608]{0:T(1024)(128)(4,1)}), s8[4194304]{0:T(1024)(128)(4,1)S(1)}, s32[]{:S(2)}) async-start(s8[8388608]{0:T(1024)(128)(4,1)} %bitcast.242), calls=%async_computation.3 | async-start | bytes 8388608
  34.5 4.1 slice-start.1
  94.4 9.5 %copy-start.6 = (s32[2]{0:T(128)S(1)}, s32[2]{0:T(128)}, u32[]{:S(2)}) copy-start(s32[2]{0:T(128)} %param.15) | copy-start | bytes 28
  94.4 9.5 %copy-start.5 = (s32[2,16]{1,0:T(2,128)S(1)}, s32[2,16]{1,0:T(2,128)}, u32[]{:S(2)}) copy-start(s32[2,16]{1,0:T(2,128)} %param.13) | copy-start | bytes 388
  94.4 9.6 %copy-start.4 = (s32[2,4,16]{2,1,0:T(4,128)S(1)}, s32[2,4,16]{2,1,0:T(4,128)}, u32[]{:S(2)}) copy-start(s32[2,4,16]{2,1,0:T(4,128)} %param.14) | copy-start | bytes 1540
  94.5 10.8 %copy-start.2 = (bf16[8,256,128]{2,1,0:T(8,128)(2,1)S(1)}, bf16[8,256,128]{2,1,0:T(8,128)(2,1)}, u32[]{:S(2)}) copy-start(bf16[8,256,128]{2,1,0:T(8,128)(2,1)} %param.11) | copy-start | bytes 1572868
  100.1 7.3 %collective-permute-start = (f32[2,2,2,512]{3,1,0,2:T(2,128)S(1)}, f32[2,2,2,512]{3,1,0,2:T(2,128)S(1)}, u32[]{:S(2)}, u32[]{:S(2)}) collective-permute-start(f32[2,2,2,512]{3,1,0,2:T(2,128)S(1)} %get-tuple-element.113), channel_id=1, source_target_pairs={{0,1},{1,2},{2,3},{4,5},{5,6},{6,7},{8,9},{9,10},{10,11},{12,13},{... | collective-permute-start | bytes 49160 | tf_op jit(solution)/shard_map/ppermute | solution.py:25
  102.4 5.2 %collective-permute-start.1 = (f32[2,2,2,512]{3,1,0,2:T(2,128)S(1)}, f32[2,2,2,512]{3,1,0,2:T(2,128)S(1)}, u32[]{:S(2)}, u32[]{:S(2)}) collective-permute-start(f32[2,2,2,512]{3,1,0,2:T(2,128)S(1)} %get-tuple-element.114), channel_id=1, source_target_pairs={{1,0},{2,1},{3,2},{5,4},{6,5},{7,6},{9,8},{10,9},{11,10},{13,12},{... | collective-permute-start | bytes 49160 | tf_op jit(solution)/shard_map/ppermute | solution.py:27
  365.9 135.3 %copy-start.1 = (bf16[8,256,128]{2,1,0:T(8,128)(2,1)S(1)}, bf16[8,256,128]{2,1,0:T(8,128)(2,1)}, u32[]{:S(2)}) copy-start(bf16[8,256,128]{2,1,0:T(8,128)(2,1)} %param.12) | copy-start | bytes 1572868
  371.5 127.9 %all-reduce.2.cloned.1.call-start = ((), (), s32[]{:S(2)}) async-start(), calls=%async_computation.2 | async-start | bytes 1048576 | tf_op jit(solution)/shard_map/psum | solution.py:151
Sparse Core Ops, SparseCore 0:
  371.7 92.2 reduce-scatter.1
  466.4 32.9 all-reduce.1
where the time goes:
time: 515 us; the launch traced here: 509 us
  matrix products  203 us (39%)
  local copies, waits for them, and re-layouts  133 us (26%)
  waiting for transfers between devices  128 us (25%)
  other arithmetic  26.5 us (5%)
  between operations  14.2 us (3%)
    reduce_scatter x1, waiting for transfers between devices, local(): lax.psum_scatter(bank_terms, 'chan', scatter_dimension=0, tiled=True)  92.4 us
    dot_general x2, matrix products, per_channel(): jnp.einsum('tijk,tijsuv->ksuv', hits_one, contrib, precision=lax.Precisio...  86.2 us
    dot_general x18, matrix products, contract_rows(): jnp.einsum('...kq,...qp->...kp', vectors, matrix, precision=lax.Precision...  84.8 us
    transpose x2, local copies, waits for them, and re-layouts, per_channel(): jnp.einsum('tijsuy,ijvy->tijsuv', formed, right_one, preferred_element_ty...  79.8 us
    psum x1, waiting for transfers between devices, local(): result = lax.psum(shares, 'tm')  35.4 us
    dot_general x2, matrix products, per_channel(): jnp.einsum('tijsuy,ijvy->tijsuv', formed, right_one, preferred_element_ty...  31.8 us
    dynamic_slice x4, local copies, waits for them, and re-layouts, local(): lax.scan(per_channel, start_banks, (pieces, left_groups, right_groups, ba...  28.4 us
    another operation x2, local copies, waits for them, and re-layouts, calibrate(): return jnp.stack([out_re, out_im], axis=-3).astype(jnp.bfloat16)  13.8 us
  transfers between devices with their start and end apart: 4, of which 3 were waited for; matrix products, arithmetic and copies ran while one was open for 1% of the time, Pallas kernels for 0%

commit v1 on v0

v1 whole, which is shorter than its diff:
```python
import functools

import jax
import jax.numpy as jnp
from jax import lax
from jax.experimental import pallas as pl
from jax.experimental.pallas import tpu as pltpu
from jax.sharding import PartitionSpec as P

N = 512
BLK = 128
BEAMS = 256
BANKS = 8
NWEIGHT = 8
ITERS = 6
HW = 2
GROUPS = N // BLK
GAINS_VMEM = 52 * 1024 * 1024
PREPARE_VMEM = 16 * 1024 * 1024
CALIBRATE_VMEM = 40 * 1024 * 1024
PRODUCTS_VMEM = 24 * 1024 * 1024

epsilon = 1e-06


def split_bf16(value):
    high = value.astype(jnp.bfloat16)
    low = (value - high.astype(jnp.float32)).astype(jnp.bfloat16)
    return high, low


GROUP = 2


def gains_kernel(vis_hbm, mod_hbm, out_ref, vis, mod, *scratch, channels, intervals, rows):
    count = channels * intervals // GROUP
    matrices, powers, (first, arrived) = scratch[:count], scratch[count : 2 * count], scratch[2 * count :]
    zero = jnp.zeros((8, N), jnp.float32)

    def place(group, k):
        return divmod(group * GROUP + k, intervals)

    def fetch(group, k):
        c, t = place(group, k)
        return (
            pltpu.make_async_copy(vis_hbm.at[c, t], vis.at[c, t], arrived.at[0, c, t]),
            pltpu.make_async_copy(mod_hbm.at[c, t], mod.at[c, t], arrived.at[1, c, t]),
        )

    def request(group):
        for k in range(GROUP):
            for copy in fetch(group, k):
                copy.start()

    request(0)

    def build(group, k, start, sums):
        c, t = place(group, k)
        at = pl.ds(start, rows)
        vis_re = vis[c, t, 0, at, :].astype(jnp.float32)
        vis_im = vis[c, t, 1, at, :].astype(jnp.float32)
        mod_re = mod[c, t, 0, at, :].astype(jnp.float32)
        mod_im = mod[c, t, 1, at, :].astype(jnp.float32)
        parts = (
            mod_re * vis_re + mod_im * vis_im,
            mod_im * vis_re - mod_re * vis_im,
            mod_re * mod_re + mod_im * mod_im,
        )
        out = []
        for index, part in enumerate(parts):
            if index < 2:
                matrices[group][k, pl.ds(index * N + start, rows), :] = part.astype(jnp.bfloat16)
            else:
                powers[group][k, at, :] = part
            out.append(sums[index] + jnp.sum(part.reshape(rows // 8, 8, N), axis=0))
        return tuple(out)

    def first_gains(group, k, sums):
        num_re, num_im, power = (jnp.sum(part, axis=0, keepdims=True) for part in sums)
        power = power + epsilon
        first[group, k, 0:1, :] = num_re / power
        first[group, k, 1:2, :] = num_im / power

    def build_in_pieces(group):
        for k in range(GROUP):
            sums = (zero, zero, zero)
            for start in range(0, N, rows):
                sums = build(group, k, start, sums)
                if start + rows == N:
                    first_gains(group, k, sums)
                yield

    row = lax.broadcasted_iota(jnp.int32, (8, N), 0)

    def slab(*entries):
        value = jnp.zeros((8, N), jnp.float32)
        for position, entry in enumerate(entries):
            value = jnp.where(row == position, entry.astype(jnp.float32), value)
        return value.astype(jnp.bfloat16)

    def spread(gain_re, gain_im):
        magnitude = gain_re * gain_re + gain_im * gain_im
        return [
            jnp.broadcast_to(magnitude[:, i * BLK : (i + 1) * BLK], (BLK, BLK)).T for i in range(GROUPS)
        ]

    def products(group, k, gain, tiles):
        gain_re, gain_im = gain
        re_high, re_low = split_bf16(gain_re)
        im_high, im_low = split_bf16(gain_im)
        left = slab(re_high, re_low, im_high, im_low)
        right = slab(-im_high, -im_low, re_high, re_low)
        num = jnp.dot(
            jnp.concatenate([left, right], axis=1), matrices[group][k], preferred_element_type=jnp.float32
        )
        denominator = []
        for j in range(GROUPS):
            total = zero[:, :BLK]
            for i in range(GROUPS):
                block = powers[group][k, i * BLK : (i + 1) * BLK, j * BLK : (j + 1) * BLK]
                total = total + jnp.sum((block * tiles[i]).reshape(BLK // 8, 8, BLK), axis=0)
            denominator.append(jnp.sum(total, axis=0, keepdims=True))
        return num, jnp.concatenate(denominator, axis=1) + epsilon

    def update(index, gain, num, denominator):
        new_re = (num[0:1] + num[1:2]) / denominator
        new_im = (num[2:3] + num[3:4]) / denominator
        if index % 2 == 1:
            return 0.5 * (new_re + gain[0]), 0.5 * (new_im + gain[1])
        return new_re, new_im

    def iterate(group, beside):
        gains = [(first[group, k, 0:1, :], first[group, k, 1:2, :]) for k in range(GROUP)]
        tiles = [spread(*gain) for gain in gains]
        waiting = None
        for index in range(1, ITERS):
            for k in range(GROUP):
                found = products(group, k, gains[k], tiles[k])
                beside()
                if waiting is not None:
                    before, at, values = waiting
                    gains[at] = update(before, gains[at], *values)
                    tiles[at] = spread(*gains[at])
                waiting = (index, k, found)
        before, at, values = waiting
        gains[at] = update(before, gains[at], *values)
        return gains

    for k in range(GROUP):
        for copy in fetch(0, k):
            copy.wait()
        if k + 1 < count:
            request(k + 1)

        def chunk(index, sums, k=k):
            return build(0, k, pl.multiple_of(index * rows, rows), sums)

        first_gains(0, k, lax.fori_loop(0, N // rows, chunk, (zero, zero, zero), unroll=2))

    for group in range(count):
        later = iter(())
        if group + 1 < count:
            for k in range(GROUP):
                for copy in fetch(group + 1, k):
                    copy.wait()
            if group + 1 + GROUP < count:
                request(group + 1 + GROUP)
            later = build_in_pieces(group + 1)
        share = -(-(N // rows) // (ITERS - 1))

        def beside():
            for _ in range(share):
                next(later, None)

        for k, (gain_re, gain_im) in enumerate(iterate(group, beside)):
            c, t = place(group, k)
            first_re = gain_re[:, :1]
            first_im = gain_im[:, :1]
            divisor = jnp.maximum(jnp.sqrt(first_re * first_re + first_im * first_im), 1.0)
            unit_re = first_re / divisor
            unit_im = -first_im / divisor
            out_ref[c, t, 0:1, :] = gain_re * unit_re - gain_im * unit_im
            out_ref[c, t, 1:2, :] = gain_re * unit_im + gain_im * unit_re


def referenced_gains(visibilities, model):
    channels, intervals = visibilities.shape[:2]
    there = pl.BlockSpec(memory_space=pltpu.HBM)
    return pl.pallas_call(
        functools.partial(gains_kernel, channels=channels, intervals=intervals, rows=32),
        in_specs=[there, there],
        out_specs=pl.BlockSpec(memory_space=pltpu.VMEM),
        out_shape=jax.ShapeDtypeStruct((channels, intervals, 2, N), jnp.float32),
        scratch_shapes=[
            pltpu.VMEM(visibilities.shape, jnp.bfloat16),
            pltpu.VMEM(model.shape, jnp.bfloat16),
        ]
        + [pltpu.VMEM((GROUP, 2 * N, N), jnp.bfloat16)] * (channels * intervals // GROUP)
        + [pltpu.VMEM((GROUP, N, N), jnp.float32)] * (channels * intervals // GROUP)
        + [
            pltpu.VMEM((channels * intervals // GROUP, GROUP, 8, N), jnp.float32),
            pltpu.SemaphoreType.DMA((2, channels, intervals)),
        ],
        compiler_params=pltpu.CompilerParams(vmem_limit_bytes=GAINS_VMEM),
        cost_estimate=pl.CostEstimate(
            flops=channels * intervals * N * N * 60, bytes_accessed=channels * intervals * N * N * 8, transcendentals=0
        ),
        name="gains",
    )(visibilities, model)


ROWS = (96, 96, 64)


PIECE = 32
PIECES = BLK // PIECE
CELLS = 2 * PIECES


def prepare_kernel(right_ref, table):
    for w in range(NWEIGHT):
        table[w * BLK : (w + 1) * BLK, :] = right_ref[w].astype(jnp.float32).T.astype(jnp.bfloat16)


def calibrate_kernel(
    weight_ref, target_ref, width_ref, place_ref,
    vis_hbm, mid_ref, low_ref, high_ref, left_ref, table, *refs, channels, intervals, all_intervals,
):
    send, keep = refs[:2]
    own_cells, refs = refs[2 : 2 + CELLS], refs[2 + CELLS :]
    cells, refs = refs[:CELLS], refs[CELLS:]
    vis, inverse, down_even, down_odd, arrived = refs[:5]
    steps = channels * intervals

    def fetch(step):
        return pltpu.make_async_copy(
            vis_hbm.at[step // intervals, step % intervals], vis.at[step], arrived.at[step]
        )

    for step in range(2):
        fetch(step).start()

    def spread(at, down):
        for part in range(2):
            for i in range(GROUPS):
                span = slice(i * BLK, (i + 1) * BLK)
                down[part, span, :] = jnp.broadcast_to(inverse[at, part : part + 1, span], (BLK, BLK)).T

    for channel in range(channels):
        width = width_ref[channel]
        for interval in range(intervals):
            smooth = jnp.zeros((2, N), jnp.float32)
            count = jnp.float32(0)
            for offset in range(-HW, HW + 1):
                at = place_ref[0] + interval + offset
                inside = ((abs(offset) <= width) & (at >= 0) & (at < all_intervals)).astype(jnp.float32)
                spot = interval + offset
                if spot < 0:
                    value = low_ref[channel, spot + HW]
                elif spot >= intervals:
                    value = high_ref[channel, spot - intervals]
                else:
                    value = mid_ref[channel, spot]
                smooth = smooth + inside * value
                count = count + inside
            smooth = smooth / count
            squares = smooth * smooth
            denominator = jnp.maximum(squares[0:1] + squares[1:2], 1.0)
            at = channel * intervals + interval
            inverse[at, 0:1, :] = smooth[0:1] / denominator
            inverse[at, 1:2, :] = -smooth[1:2] / denominator
    for array in cells:
        array[...] = jnp.zeros_like(array)
    spread(0, down_even)

    def add_later(waiting):
        cell, piece, value_re, value_im = waiting
        cells[piece][cell] += value_re
        cells[PIECES + piece][cell] += value_im

    def calibrate(step, down, next_down):
        channel = step // intervals
        interval = step % intervals
        spread(jnp.minimum(step + 1, steps - 1), next_down)
        waiting = []
        for i in range(GROUPS):
            cell = [
                weight_ref[channel, block] * BANKS + target_ref[channel, interval * GROUPS * GROUPS + block]
                for block in range(i * GROUPS, (i + 1) * GROUPS)
            ]
            for j in range(GROUPS):
                span = slice(j * BLK, (j + 1) * BLK)
                for piece in range(PIECES):
                    at = slice(i * BLK + piece * PIECE, i * BLK + (piece + 1) * PIECE)
                    row_re = down[0, at, :]
                    row_im = down[1, at, :]
                    vis_re = vis[step, 0, at, span].astype(jnp.float32)
                    vis_im = vis[step, 1, at, span].astype(jnp.float32)
                    col_re = inverse[step, 0:1, span]
                    col_im = inverse[step, 1:2, span]
                    left_re = row_re * vis_re - row_im * vis_im
                    left_im = row_re * vis_im + row_im * vis_re
                    out_re = left_re * col_re + left_im * col_im
                    out_im = left_im * col_re - left_re * col_im
                    if len(waiting) == 2:
                        add_later(waiting.pop(0))
                    waiting.append((cell[j], piece, out_re, out_im))
        for entry in waiting:
            add_later(entry)

    def pair(turn, carry):
        step = 2 * turn
        fetch(step).wait()
        fetch(step + 1).wait()
        calibrate(step, down_even, down_odd)
        calibrate(step + 1, down_odd, down_even)
        return carry

    for step in range(2, steps):
        fetch(step).start()
    lax.fori_loop(0, steps // 2, pair, 0)
    four = BANKS // 2

    def cell_of(turn, w):
        own = w * BANKS + place_ref[3 + four + turn]
        for array, out in zip(cells, own_cells):
            out[w * four + turn] = array[own]
        return w * BANKS + place_ref[3 + turn]

    bank_products(place_ref, cells, cell_of, left_ref, table, send, keep, *refs[5:])


def own_products_kernel(place_ref, left_ref, table, *refs):
    def cell_of(turn, w):
        return w * (BANKS // 2) + turn

    bank_products(place_ref, refs[:CELLS], cell_of, left_ref, table, *refs[CELLS:])


def bank_products(
    place_ref, cells, cell_of, left_ref, table, send, keep, formed_even, formed_odd, product_even, product_odd
):
    count = BANKS // 2
    core = place_ref[1]
    across = place_ref[2]
    formed = (formed_even, formed_odd)
    product = (product_even, product_odd)

    def left_product(turn, w):
        cell = cell_of(turn, w)
        pair = jnp.concatenate(
            [
                jnp.concatenate([array[cell] for array in cells[:PIECES]], axis=0),
                jnp.concatenate([array[cell] for array in cells[PIECES:]], axis=0),
            ],
            axis=1,
        )
        high, low = split_bf16(pair)
        left = left_ref[w]
        beams = jnp.dot(
            jnp.concatenate([left, left], axis=1),
            jnp.concatenate([high, low], axis=0),
            preferred_element_type=jnp.float32,
        ).astype(jnp.bfloat16)
        formed[turn % 2][:BEAMS, w * BLK : (w + 1) * BLK] = beams[:, :BLK]
        formed[turn % 2][BEAMS:, w * BLK : (w + 1) * BLK] = beams[:, BLK:]

    def right_product(turn):
        product[turn % 2][...] = jnp.dot(
            formed[turn % 2][...], table[...], preferred_element_type=jnp.float32
        )

    def hand_out(turn):
        for part, out in ((1 - core, send), (core, keep)):
            start = 0
            for group, size in enumerate(rows // 2 for rows in ROWS):
                for away, half in ((0, across), (1, 1 - across)) if group < 2 else ((0, 0), (1, 1)):
                    at = part * BEAMS + start + half * size
                    out[turn, start + away * size : start + (away + 1) * size, :] = product[turn % 2][
                        pl.ds(pl.multiple_of(at, 16), size), :
                    ]
                start += 2 * size

    for turn in range(count + 1):
        if turn:
            right_product(turn - 1)
        if turn < count:
            for w in range(NWEIGHT):
                left_product(turn, w)
        if turn:
            hand_out(turn - 1)


SCALARS = pl.BlockSpec(memory_space=pltpu.SMEM)
VECTORS = pl.BlockSpec(memory_space=pltpu.VMEM)


def beam_products(weight_index, target_bank, widths, place, all_intervals, visibilities, mid, low, high, beam_left, beam_right):
    channels, intervals = visibilities.shape[:2]
    steps = channels * intervals
    table = pl.pallas_call(
        prepare_kernel,
        in_specs=[VECTORS],
        out_specs=VECTORS,
        out_shape=jax.ShapeDtypeStruct((NWEIGHT * BLK, BEAMS), jnp.bfloat16),
        compiler_params=pltpu.CompilerParams(vmem_limit_bytes=PREPARE_VMEM),
        cost_estimate=pl.CostEstimate(flops=10**6, bytes_accessed=1024 * 1024, transcendentals=0),
        name="prepare",
    )(lax.optimization_barrier((beam_right, mid))[0])
    banks_shape = [jax.ShapeDtypeStruct((BANKS // 2, BEAMS, BEAMS), jnp.float32)] * 2
    product_scratch = [pltpu.VMEM((2 * BEAMS, NWEIGHT * BLK), jnp.bfloat16)] * 2 + [
        pltpu.VMEM((2 * BEAMS, BEAMS), jnp.float32)
    ] * 2
    send_away, keep_away, *cells = pl.pallas_call(
        functools.partial(
            calibrate_kernel, channels=channels, intervals=intervals, all_intervals=all_intervals
        ),
        in_specs=[SCALARS] * 4 + [pl.BlockSpec(memory_space=pltpu.HBM)] + [VECTORS] * 5,
        out_specs=[VECTORS] * (2 + CELLS),
        scratch_shapes=[pltpu.VMEM((NWEIGHT * BANKS, PIECE, BLK), jnp.float32)] * CELLS
        + [
            pltpu.VMEM((steps, 2, N, N), jnp.bfloat16),
            pltpu.VMEM((steps, 8, N), jnp.float32),
            pltpu.VMEM((2, N, BLK), jnp.float32),
            pltpu.VMEM((2, N, BLK), jnp.float32),
            pltpu.SemaphoreType.DMA((steps,)),
        ]
        + product_scratch,
        out_shape=banks_shape
        + [jax.ShapeDtypeStruct((NWEIGHT * BANKS // 2, PIECE, BLK), jnp.float32)] * CELLS,
        compiler_params=pltpu.CompilerParams(vmem_limit_bytes=CALIBRATE_VMEM),
        cost_estimate=pl.CostEstimate(
            flops=2 * 10**9, bytes_accessed=steps * N * N * 8, transcendentals=0
        ),
        name="calibrate",
    )(
        weight_index, target_bank.reshape(channels, -1), widths, place,
        visibilities, mid, low, high, beam_left, table,
    )
    send_own, keep_own = pl.pallas_call(
        own_products_kernel,
        in_specs=[SCALARS] + [VECTORS] * (2 + CELLS),
        out_specs=[VECTORS] * 2,
        scratch_shapes=product_scratch,
        out_shape=banks_shape,
        compiler_params=pltpu.CompilerParams(vmem_limit_bytes=PRODUCTS_VMEM),
        cost_estimate=pl.CostEstimate(
            flops=2 * 10**9, bytes_accessed=2 * 1024 * 1024, transcendentals=0
        ),
        name="products",
    )(place, beam_left, table, *cells)
    return send_away, keep_away, send_own, keep_own


SLOTS = tuple((1 - (p >> 2)) | ((p & 3) << 1) for p in range(BANKS))


def swap(value, axis, mask):
    count = lax.axis_size(axis)
    return lax.ppermute(value, axis, [(i, i ^ mask) for i in range(count)])


def assemble_kernel(place_ref, mine, other, out, done):
    core = place_ref[1]
    across = place_ref[2]
    half_p, half_q = ROWS[0] // 2, ROWS[1] // 2
    copies = []
    for part, rows in ((core, mine), (1 - core, other)):
        base = part * BEAMS
        pieces = [
            (at + half * size, size)
            for half in (across, 1 - across)
            for at, size in ((0, half_p), (ROWS[0], half_q))
        ] + [(ROWS[0] + ROWS[1], ROWS[2])]
        start = 0
        for at, size in pieces:
            copies.append(
                pltpu.make_async_copy(
                    rows.at[start : start + size],
                    out.at[pl.ds(pl.multiple_of(base + at, 16), size)],
                    done.at[len(copies)],
                )
            )
            start += size
    for copy in copies:
        copy.start()
    for copy in copies:
        copy.wait()


def reduce_banks(place, send_away, keep_away, send_own, keep_own):
    four = BANKS // 2
    half_p, half_q = ROWS[0] // 2, ROWS[1] // 2
    q_at = 2 * half_p
    q_half = q_at + half_q
    r_at = q_half + half_q
    got_away = swap(send_away, "tm", 1)
    got_own = swap(send_own, "tm", 1)

    def away(low, high):
        return keep_away[:, low:high] + got_away[:, low:high]

    def own(low, high):
        return keep_own[:, low:high] + got_own[:, low:high]

    p_got = swap(away(0, q_at), "chan", 1)
    q_got = swap(jnp.concatenate([away(q_half, r_at), own(q_half, r_at)], axis=0), "tm", 2)
    r_here = jnp.stack([own(r_at, None), away(r_at, None)], axis=1)
    r_got = [swap(r_here[k], "chan", 2 * k) for k in (3, 2, 1)]
    p_here = own(0, q_at) + p_got
    p_got = swap(p_here[:, half_p:], "tm", 2)
    p_got, *r_got = lax.optimization_barrier((p_got, *r_got))
    p_here = p_here[:, :half_p] + p_got
    q_own = own(q_at, q_half) + q_got[four:]
    q_other = away(q_at, q_half) + q_got[:four]
    q_here = q_own + swap(q_other, "chan", 1)
    r_here = r_here[0] + r_got[0] + r_got[1] + r_got[2]
    r_here = r_here[0] + swap(r_here[1], "chan", 1)
    here = jnp.concatenate([p_here, q_here], axis=1)
    z_got = [swap(here[k], "chan", 2 * k) for k in (3, 2, 1)]
    here = here[0] + z_got[0] + z_got[1] + z_got[2]
    x_got = swap(jnp.concatenate([here, r_here], axis=0), "tm", 2)
    pq = half_p + half_q
    mine = jnp.concatenate([here, x_got[:pq], r_here + x_got[pq:]], axis=0)
    other = swap(mine, "tm", 1)
    return pl.pallas_call(
        assemble_kernel,
        in_specs=[SCALARS, VECTORS, VECTORS],
        out_specs=pl.BlockSpec(memory_space=pltpu.HBM),
        out_shape=jax.ShapeDtypeStruct((2 * BEAMS, BEAMS), jnp.float32),
        scratch_shapes=[pltpu.SemaphoreType.DMA((10,))],
        compiler_params=pltpu.CompilerParams(vmem_limit_bytes=PREPARE_VMEM),
        name="assemble",
    )(place, mine, other)


def reduce_plain(send_first, keep_first, send_last, keep_last):
    keep = jnp.concatenate([keep_first, keep_last])
    send = jnp.concatenate([send_first, send_last])
    banks = jnp.stack([keep, send], axis=1).reshape((BANKS * 2 * BEAMS, BEAMS))
    shares = lax.psum_scatter(banks, "chan", scatter_dimension=0, tiled=True)
    return lax.psum(shares, "tm")


def neighbour_gains(gains):
    count = lax.axis_size("tm")
    odd = lax.axis_index("tm") % 2 == 1
    head = gains[:, :HW]
    tail = gains[:, gains.shape[1] - HW :]
    inner = lax.ppermute(jnp.where(odd, head, tail), "tm", [(i, i ^ 1) for i in range(count)])
    links = [(i, i + 1) for i in range(1, count - 1, 2)]
    outer = lax.ppermute(jnp.where(odd, tail, head), "tm", links + [(j, i) for i, j in links])
    return jnp.where(odd, inner, outer), jnp.where(odd, outer, inner)


def local(visibilities, model, beam_left, beam_right, weight_index, target_bank, widths):
    local_intervals = visibilities.shape[1]
    count = lax.axis_size("tm")
    tm = lax.axis_index("tm")
    chan = lax.axis_index("chan")
    one_bank_each = lax.axis_size("chan") == BANKS and count == 4
    if one_bank_each:
        place = [tm * local_intervals, tm % 2, tm // 2] + [chan ^ slot for slot in SLOTS]
    else:
        place = [tm * local_intervals, 0, 0] + list(range(BANKS))
    place = jnp.stack([jnp.asarray(entry, jnp.int32) for entry in place])
    gains = referenced_gains(visibilities, model)
    low, high = neighbour_gains(gains)
    pieces = beam_products(
        weight_index, target_bank, widths, place, count * local_intervals,
        visibilities, gains, low, high, beam_left, beam_right,
    )
    if one_bank_each:
        return reduce_banks(place, *pieces)
    return reduce_plain(*pieces)


def solution(mesh):
    return jax.shard_map(
        local,
        mesh=mesh,
        in_specs=(
            P("chan", "tm", None, None, None),
            P("chan", "tm", None, None, None),
            P(),
            P(),
            P("chan", None),
            P("chan", "tm", None),
            P("chan"),
        ),
        out_specs=P("chan", None),
        check_vma=False,
    )
```

time: 515 us -> 76.6 us (0.15); the launches traced: 509 us -> 76.4 us
  matrix products: 203 us -> 0 us
  local copies, waits for them, and re-layouts: 133 us -> 0.22 us
  waiting for transfers between devices: 128 us -> 21.5 us
  Pallas kernels: 0 us -> 29.8 us
  other arithmetic: 26.5 us -> 0.59 us
  starting transfers between devices: 3.69 us -> 23.9 us
  between operations: 14.2 us -> 0.4 us
    dot_general x22 -> x0, matrix products: 203 us -> none  [the longest x2 86.2 us: per_channel(): jnp.einsum('tijk,tijsuv->ksuv', hits_one, contrib, precision=lax.Precisio...]
    reduce_scatter x1 -> x0, waiting for transfers between devices: 92.4 us -> none  [local(): lax.psum_scatter(bank_terms, 'chan', scatter_dimension=0, tiled=True)]
    transpose x2 -> x0, local copies, waits for them, and re-layouts: 79.8 us -> none  [per_channel(): jnp.einsum('tijsuy,ijvy->tijsuv', formed, right_one, preferred_element_ty...]
    psum x1 -> x0, waiting for transfers between devices: 35.4 us -> none  [local(): result = lax.psum(shares, 'tm')]
    pallas_call x0 -> x5, Pallas kernels: none -> 29.8 us  [the longest x1 14.1 us: referenced_gains(): pl.pallas_call(functools.partial(gains_kernel, channels=channels, interva...]
    dynamic_slice x4 -> x0, local copies, waits for them, and re-layouts: 28.4 us -> none  [local(): lax.scan(per_channel, start_banks, (pieces, left_groups, right_groups, ba...]
    ppermute x2 -> x17, waiting for transfers between devices: 0.21 us -> 21.5 us  [the longest x15 21.1 us: swap(): return lax.ppermute(value, axis, [(i, i ^ mask) for i in range(count)])]
    ppermute x2 -> x17, starting transfers between devices: 3.65 us -> 23.9 us  [the longest x15 18.7 us: swap(): return lax.ppermute(value, axis, [(i, i ^ mask) for i in range(count)])]
  transfers between devices with their start and end apart: 4 -> 17, of which waited for: 3 -> 11; matrix products, arithmetic and copies ran while one was open for 1% -> 1% of each run, Pallas kernels for 0% -> 5%
where the time goes in v1:
time: 76.6 us; the launch traced here: 76.4 us
  Pallas kernels  29.8 us (39%)
  starting transfers between devices  23.9 us (31%)
  waiting for transfers between devices  21.5 us (28%)
    ppermute x15, waiting for transfers between devices, swap(): return lax.ppermute(value, axis, [(i, i ^ mask) for i in range(count)])  21.1 us
    ppermute x15, starting transfers between devices, swap(): return lax.ppermute(value, axis, [(i, i ^ mask) for i in range(count)])  18.7 us
    pallas_call x1, Pallas kernels, referenced_gains(): pl.pallas_call(functools.partial(gains_kernel, channels=channels, interva...  14.1 us
    pallas_call x1, Pallas kernels, beam_products(): pl.pallas_call(functools.partial(calibrate_kernel, channels=channels, int...  10.6 us
    ppermute x1, starting transfers between devices, neighbour_gains(): lax.ppermute(jnp.where(odd, head, tail), 'tm', [(i, i ^ 1) for i in range...  4.38 us
    pallas_call x1, Pallas kernels, beam_products(): pl.pallas_call(own_products_kernel, in_specs=[SCALARS] + [VECTORS] * (2 +...  3.45 us
  transfers between devices with their start and end apart: 17, of which 11 were waited for; matrix products, arithmetic and copies ran while one was open for 1% of the time, Pallas kernels for 5%

profile of v1, /device:TPU:0, one launch (start us, length us, event | category | flops | bytes accessed | tf_op | source)
XLA Modules:
  0.0 76.4 jit_solution(9564154426009912568)
XLA Ops:
  0.0 14.1 %gains.1.mid_ref = f32[2,4,2,512]{3,2,1,0:T(2,128)S(1)} custom-call(bf16[2,4,2,512,512]{4,3,2,1,0:T(8,128)(2,1)} %vis_hbm.3, bf16[2,4,2,512,512]{4,3,2,1,0:T(8,128)(2,1)} %mod_hbm.1), custom_call_target="tpu_custom_call" | custom-call | flops 125829120 | bytes 16777216 | tf_op jit(solution)/shard_map/gains/pallas_call | solution.py:189
  14.2 0.8 %collective-permute-start.1 = (f32[2,2,2,512]{3,2,1,0:T(2,128)S(1)}, f32[2,2,2,512]{3,2,1,0:T(2,128)S(1)}, u32[]{:S(2)}, u32[]{:S(2)}) collective-permute-start(f32[2,2,2,512]{3,2,1,0:T(2,128)S(1)} %get-tuple-element.47), channel_id=1, source_target_pairs={{1,2},{2,1},{5,6},{6,5},{9,10},{10,9},{13,14},{14,13},{17,18},{18,... | collective-permute-start | bytes 49160 | tf_op jit(solution)/shard_map/ppermute | solution.py:552
  15.0 4.4 %collective-permute-start = (f32[2,2,2,512]{3,2,1,0:T(2,128)S(1)}, f32[2,2,2,512]{3,2,1,0:T(2,128)S(1)}, u32[]{:S(2)}, u32[]{:S(2)}) collective-permute-start(f32[2,2,2,512]{3,2,1,0:T(2,128)S(1)} %get-tuple-element.48), channel_id=1, source_target_pairs={{0,1},{1,0},{2,3},{3,2},{4,5},{5,4},{6,7},{7,6},{8,9},{9,8},{10,11... | collective-permute-start | bytes 49160 | tf_op jit(solution)/shard_map/ppermute | solution.py:550
  19.4 0.1 reshape.3.target_ref
  19.5 0.1 stack.56.place_ref
  19.6 0.2 prepare.1.table
  19.8 0.4 collective-permute-done
  20.3 10.6 %calibrate.1 = (f32[4,256,256]{2,1,0:T(8,128)S(1)}, f32[4,256,256]{2,1,0:T(8,128)S(1)}, f32[32,32,128]{2,1,0:T(8,128)S(1)}, f32[32,32,128]{2,1,0:T(8,128)S(1)}, ...) custom-call(s32[2,16]{1,0:T(2,128)S(1)} %copy-done.2, ...), custom_call_target="tpu_custom_call" | custom-call | flops 2000000000 | bytes 16777216 | tf_op jit(solution)/shard_map/calibrate/pallas_call | solution.py:414
  30.9 0.4 collective-permute-start.3
  31.3 3.4 %products.1 = (f32[4,256,256]{2,1,0:T(8,128)S(1)}, f32[4,256,256]{2,1,0:T(8,128)S(1)}) custom-call(s32[11]{0:T(128)S(1)} %stack.56.place_ref, bf16[8,256,128]{2,1,0:T(8,128)(2,1)S(1)} %copy-done, bf16[1024,256]{1,0:T(8,128)(2,1)S(1)} %prepare.1.table, f32[32,32,128]{2,1,0:T(8,128)S(1)} %get-tuple-element.23.refs_0_, ...), custom_call_target="tpu_custom_call" | custom-call | flops 2000000000 | bytes 2097152 | tf_op jit(solution)/shard_map/products/pallas_call | solution.py:440
  34.8 0.2 collective-permute-start.2
  35.0 1.6 %collective-permute-start.4 = (f32[4,96,256]{2,1,0:T(8,128)S(1)}, f32[4,96,256]{2,1,0:T(8,128)S(1)}, u32[]{:S(2)}, u32[]{:S(2)}) collective-permute-start(f32[4,96,256]{2,1,0:T(8,128)S(1)} %slice_add_fusion), channel_id=1, source_target_pairs={{0,4},{4,0},{8,12},{12,8},{16,20},{20,16},{24,28},{28,24},{1,5},{5... | collective-permute-start | bytes 1179656 | tf_op jit(solution)/shard_map/ppermute | solution.py:460
  36.6 0.9 %collective-permute-done.2 = f32[4,256,256]{2,1,0:T(8,128)S(1)} collective-permute-done((f32[4,256,256]{2,1,0:T(8,128)S(1)}, f32[4,256,256]{2,1,0:T(8,128)S(1)}, u32[]{:S(2)}, u32[]{:S(2)}) %collective-permute-start.2) | collective-permute-done | bytes 1048608 | tf_op jit(solution)/shard_map/ppermute | solution.py:460
  37.6 1.8 %collective-permute-start.9 = (f32[8,48,256]{2,1,0:T(8,128)S(1)}, f32[8,48,256]{2,1,0:T(8,128)S(1)}, u32[]{:S(2)}, u32[]{:S(2)}) collective-permute-start(f32[8,48,256]{2,1,0:T(8,128)S(1)} %pad_maximum_fusion), channel_id=1, source_target_pairs={{0,2},{1,3},{2,0},{3,1},{4,6},{5,7},{6,4},{7,5},{8,10},{9,11},{10,... | collective-permute-start | bytes 1179656 | tf_op jit(solution)/shard_map/ppermute | solution.py:460
  39.5 1.6 %collective-permute-start.8 = (f32[2,64,256]{2,1,0:T(8,128)S(1)}, f32[2,64,256]{2,1,0:T(8,128)S(1)}, u32[]{:S(2)}, u32[]{:S(2)}) collective-permute-start(f32[2,64,256]{2,1,0:T(8,128)S(1)} %get-tuple-element.39), channel_id=1, source_target_pairs={{0,8},{4,12},{8,0},{12,4},{16,24},{20,28},{24,16},{28,20},{1,9},{5... | collective-permute-start | bytes 393224 | tf_op jit(solution)/shard_map/ppermute | solution.py:460
  41.1 2.5 %collective-permute-start.6 = (f32[2,64,256]{2,1,0:T(8,128)S(1)}, f32[2,64,256]{2,1,0:T(8,128)S(1)}, u32[]{:S(2)}, u32[]{:S(2)}) collective-permute-start(f32[2,64,256]{2,1,0:T(8,128)S(1)} %get-tuple-element.40), channel_id=1, source_target_pairs={{0,24},{4,28},{8,16},{12,20},{16,8},{20,12},{24,0},{28,4},{1,25},{... | collective-permute-start | bytes 393224 | tf_op jit(solution)/shard_map/ppermute | solution.py:460
  43.6 0.1 collective-permute-start.7
  43.7 2.8 %collective-permute-done.4 = f32[4,96,256]{2,1,0:T(8,128)S(1)} collective-permute-done((f32[4,96,256]{2,1,0:T(8,128)S(1)}, f32[4,96,256]{2,1,0:T(8,128)S(1)}, u32[]{:S(2)}, u32[]{:S(2)}) %collective-permute-start.4) | collective-permute-done | bytes 393248 | tf_op jit(solution)/shard_map/ppermute | solution.py:460
  46.6 1.7 %collective-permute-start.5 = (f32[4,48,256]{2,1,0:T(8,128)S(1)}, f32[4,48,256]{2,1,0:T(8,128)S(1)}, u32[]{:S(2)}, u32[]{:S(2)}) collective-permute-start(f32[4,48,256]{2,1,0:T(8,128)S(1)} %slice.141), channel_id=1, source_target_pairs={{0,2},{1,3},{2,0},{3,1},{4,6},{5,7},{6,4},{7,5},{8,10},{9,11},{10,... | collective-permute-start | bytes 589832 | tf_op jit(solution)/shard_map/ppermute | solution.py:460
  48.2 0.8 %collective-permute-done.9 = f32[8,48,256]{2,1,0:T(8,128)S(1)} collective-permute-done((f32[8,48,256]{2,1,0:T(8,128)S(1)}, f32[8,48,256]{2,1,0:T(8,128)S(1)}, u32[]{:S(2)}, u32[]{:S(2)}) %collective-permute-start.9) | collective-permute-done | bytes 393248 | tf_op jit(solution)/shard_map/ppermute | solution.py:460
  49.1 1.6 %collective-permute-start.10 = (f32[4,48,256]{2,1,0:T(8,128)S(1)}, f32[4,48,256]{2,1,0:T(8,128)S(1)}, u32[]{:S(2)}, u32[]{:S(2)}) collective-permute-start(f32[4,48,256]{2,1,0:T(8,128)S(1)} %slice_add_fusion.4), channel_id=1, source_target_pairs={{0,4},{4,0},{8,12},{12,8},{16,20},{20,16},{24,28},{28,24},{1,5},{5... | collective-permute-start | bytes 589832 | tf_op jit(solution)/shard_map/ppermute | solution.py:460
  50.8 4.8 %collective-permute-done.7 = f32[2,64,256]{2,1,0:T(8,128)S(1)} collective-permute-done((f32[2,64,256]{2,1,0:T(8,128)S(1)}, f32[2,64,256]{2,1,0:T(8,128)S(1)}, u32[]{:S(2)}, u32[]{:S(2)}) %collective-permute-start.7) | collective-permute-done | bytes 131104 | tf_op jit(solution)/shard_map/ppermute | solution.py:460
  55.6 1.6 %collective-permute-start.14 = (f32[64,256]{1,0:T(8,128)S(1)}, f32[64,256]{1,0:T(8,128)S(1)}, u32[]{:S(2)}, u32[]{:S(2)}) collective-permute-start(f32[64,256]{1,0:T(8,128)S(1)} %slice_bitcast_fusion), channel_id=1, source_target_pairs={{0,4},{4,0},{8,12},{12,8},{16,20},{20,16},{24,28},{28,24},{1,5},{5... | collective-permute-start | bytes 196616 | tf_op jit(solution)/shard_map/ppermute | solution.py:460
  57.3 2.7 %collective-permute-start.11 = (f32[96,256]{1,0:T(8,128)S(1)}, f32[96,256]{1,0:T(8,128)S(1)}, u32[]{:S(2)}, u32[]{:S(2)}) collective-permute-start(f32[96,256]{1,0:T(8,128)S(1)} %get-tuple-element.42), channel_id=1, source_target_pairs={{0,24},{4,28},{8,16},{12,20},{16,8},{20,12},{24,0},{28,4},{1,25},{... | collective-permute-start | bytes 294920 | tf_op jit(solution)/shard_map/ppermute | solution.py:460
  60.1 1.7 %collective-permute-start.12 = (f32[96,256]{1,0:T(8,128)S(1)}, f32[96,256]{1,0:T(8,128)S(1)}, u32[]{:S(2)}, u32[]{:S(2)}) collective-permute-start(f32[96,256]{1,0:T(8,128)S(1)} %get-tuple-element.44), channel_id=1, source_target_pairs={{0,16},{4,20},{8,24},{12,28},{16,0},{20,4},{24,8},{28,12},{1,17},{... | collective-permute-start | bytes 294920 | tf_op jit(solution)/shard_map/ppermute | solution.py:460
  61.8 3.2 %collective-permute-done.11 = f32[96,256]{1,0:T(8,128)S(1)} collective-permute-done((f32[96,256]{1,0:T(8,128)S(1)}, f32[96,256]{1,0:T(8,128)S(1)}, u32[]{:S(2)}, u32[]{:S(2)}) %collective-permute-start.11) | collective-permute-done | bytes 98336 | tf_op jit(solution)/shard_map/ppermute | solution.py:460
  65.0 1.9 %collective-permute-done.13 = f32[96,256]{1,0:T(8,128)S(1)} collective-permute-done((f32[96,256]{1,0:T(8,128)S(1)}, f32[96,256]{1,0:T(8,128)S(1)}, u32[]{:S(2)}, u32[]{:S(2)}) %collective-permute-start.13) | collective-permute-done | bytes 98336 | tf_op jit(solution)/shard_map/ppermute | solution.py:460
  67.0 0.8 %collective-permute-done.12 = f32[96,256]{1,0:T(8,128)S(1)} collective-permute-done((f32[96,256]{1,0:T(8,128)S(1)}, f32[96,256]{1,0:T(8,128)S(1)}, u32[]{:S(2)}, u32[]{:S(2)}) %collective-permute-start.12) | collective-permute-done | bytes 98336 | tf_op jit(solution)/shard_map/ppermute | solution.py:460
  67.8 1.1 %collective-permute-start.15 = (f32[160,256]{1,0:T(8,128)S(1)}, f32[160,256]{1,0:T(8,128)S(1)}, u32[]{:S(2)}, u32[]{:S(2)}) collective-permute-start(f32[160,256]{1,0:T(8,128)S(1)} %pad_maximum_fusion.2), channel_id=1, source_target_pairs={{0,2},{1,3},{2,0},{3,1},{4,6},{5,7},{6,4},{7,5},{8,10},{9,11},{10,... | collective-permute-start | bytes 491528 | tf_op jit(solution)/shard_map/ppermute | solution.py:460
  68.9 4.3 %collective-permute-done.15 = f32[160,256]{1,0:T(8,128)S(1)} collective-permute-done((f32[160,256]{1,0:T(8,128)S(1)}, f32[160,256]{1,0:T(8,128)S(1)}, u32[]{:S(2)}, u32[]{:S(2)}) %collective-permute-start.15) | collective-permute-done | bytes 163872 | tf_op jit(solution)/shard_map/ppermute | solution.py:460
  73.3 1.5 %collective-permute-done.16.other = f32[256,256]{1,0:T(8,128)S(1)} collective-permute-done((f32[256,256]{1,0:T(8,128)S(1)}, f32[256,256]{1,0:T(8,128)S(1)}, u32[]{:S(2)}, u32[]{:S(2)}) %collective-permute-start.16) | collective-permute-done | bytes 262176 | tf_op jit(solution)/shard_map/ppermute | solution.py:460
  74.8 1.4 %assemble.1 = f32[512,256]{1,0:T(8,128)} custom-call(s32[11]{0:T(128)S(1)} %stack.56.place_ref, f32[256,256]{1,0:T(8,128)S(1)} %pad_maximum_fusion.1.mine, f32[256,256]{1,0:T(8,128)S(1)} %collective-permute-done.16.other), custom_call_target="tpu_custom_call" | custom-call | tf_op jit(solution)/shard_map/assemble/pallas_call | solution.py:526
  (42 shorter events, 0.8 us)
Async XLA Ops:
  0.0 19.4 %copy-start.4 = (s32[2,4,16]{2,1,0:T(4,128)S(1)}, s32[2,4,16]{2,1,0:T(4,128)}, u32[]{:S(2)}) copy-start(s32[2,4,16]{2,1,0:T(4,128)} %param.12) | copy-start | bytes 1540
  0.0 19.6 %copy-start.1 = (bf16[8,256,128]{2,1,0:T(8,128)(2,1)S(1)}, bf16[8,256,128]{2,1,0:T(8,128)(2,1)}, u32[]{:S(2)}) copy-start(bf16[8,256,128]{2,1,0:T(8,128)(2,1)} %right_ref) | copy-start | bytes 1572868
  0.0 20.2 %copy-start = (bf16[8,256,128]{2,1,0:T(8,128)(2,1)S(1)}, bf16[8,256,128]{2,1,0:T(8,128)(2,1)}, u32[]{:S(2)}) copy-start(bf16[8,256,128]{2,1,0:T(8,128)(2,1)} %left_ref.3) | copy-start | bytes 1572868
  0.0 20.3 %copy-start.2 = (s32[2,16]{1,0:T(2,128)S(1)}, s32[2,16]{1,0:T(2,128)}, u32[]{:S(2)}) copy-start(s32[2,16]{1,0:T(2,128)} %weight_ref.1) | copy-start | bytes 388
  0.0 20.3 %copy-start.3 = (s32[2]{0:T(128)S(1)}, s32[2]{0:T(128)}, u32[]{:S(2)}) copy-start(s32[2]{0:T(128)} %width_ref.1) | copy-start | bytes 28
  14.2 5.6 %collective-permute-start.1 = (f32[2,2,2,512]{3,2,1,0:T(2,128)S(1)}, f32[2,2,2,512]{3,2,1,0:T(2,128)S(1)}, u32[]{:S(2)}, u32[]{:S(2)}) collective-permute-start(f32[2,2,2,512]{3,2,1,0:T(2,128)S(1)} %get-tuple-element.47), channel_id=1, source_target_pairs={{1,2},{2,1},{5,6},{6,5},{9,10},{10,9},{13,14},{14,13},{17,18},{18,... | collective-permute-start | bytes 49160 | tf_op jit(solution)/shard_map/ppermute | solution.py:552
  15.0 5.2 %collective-permute-start = (f32[2,2,2,512]{3,2,1,0:T(2,128)S(1)}, f32[2,2,2,512]{3,2,1,0:T(2,128)S(1)}, u32[]{:S(2)}, u32[]{:S(2)}) collective-permute-start(f32[2,2,2,512]{3,2,1,0:T(2,128)S(1)} %get-tuple-element.48), channel_id=1, source_target_pairs={{0,1},{1,0},{2,3},{3,2},{4,5},{5,4},{6,7},{7,6},{8,9},{9,8},{10,11... | collective-permute-start | bytes 49160 | tf_op jit(solution)/shard_map/ppermute | solution.py:550
  30.9 4.1 %collective-permute-start.3 = (f32[4,256,256]{2,1,0:T(8,128)S(1)}, f32[4,256,256]{2,1,0:T(8,128)S(1)}, u32[]{:S(2)}, u32[]{:S(2)}) collective-permute-start(f32[4,256,256]{2,1,0:T(8,128)S(1)} %get-tuple-element.34), channel_id=1, source_target_pairs={{0,1},{1,0},{2,3},{3,2},{4,5},{5,4},{6,7},{7,6},{8,9},{9,8},{10,11... | collective-permute-start | bytes 3145736 | tf_op jit(solution)/shard_map/ppermute | solution.py:460
  34.8 2.7 %collective-permute-start.2 = (f32[4,256,256]{2,1,0:T(8,128)S(1)}, f32[4,256,256]{2,1,0:T(8,128)S(1)}, u32[]{:S(2)}, u32[]{:S(2)}) collective-permute-start(f32[4,256,256]{2,1,0:T(8,128)S(1)} %get-tuple-element.32), channel_id=1, source_target_pairs={{0,1},{1,0},{2,3},{3,2},{4,5},{5,4},{6,7},{7,6},{8,9},{9,8},{10,11... | collective-permute-start | bytes 3145736 | tf_op jit(solution)/shard_map/ppermute | solution.py:460
  35.0 11.5 %collective-permute-start.4 = (f32[4,96,256]{2,1,0:T(8,128)S(1)}, f32[4,96,256]{2,1,0:T(8,128)S(1)}, u32[]{:S(2)}, u32[]{:S(2)}) collective-permute-start(f32[4,96,256]{2,1,0:T(8,128)S(1)} %slice_add_fusion), channel_id=1, source_target_pairs={{0,4},{4,0},{8,12},{12,8},{16,20},{20,16},{24,28},{28,24},{1,5},{5... | collective-permute-start | bytes 1179656 | tf_op jit(solution)/shard_map/ppermute | solution.py:460
  37.6 11.5 %collective-permute-start.9 = (f32[8,48,256]{2,1,0:T(8,128)S(1)}, f32[8,48,256]{2,1,0:T(8,128)S(1)}, u32[]{:S(2)}, u32[]{:S(2)}) collective-permute-start(f32[8,48,256]{2,1,0:T(8,128)S(1)} %pad_maximum_fusion), channel_id=1, source_target_pairs={{0,2},{1,3},{2,0},{3,1},{4,6},{5,7},{6,4},{7,5},{8,10},{9,11},{10,... | collective-permute-start | bytes 1179656 | tf_op jit(solution)/shard_map/ppermute | solution.py:460
  39.5 11.3 %collective-permute-start.8 = (f32[2,64,256]{2,1,0:T(8,128)S(1)}, f32[2,64,256]{2,1,0:T(8,128)S(1)}, u32[]{:S(2)}, u32[]{:S(2)}) collective-permute-start(f32[2,64,256]{2,1,0:T(8,128)S(1)} %get-tuple-element.39), channel_id=1, source_target_pairs={{0,8},{4,12},{8,0},{12,4},{16,24},{20,28},{24,16},{28,20},{1,9},{5... | collective-permute-start | bytes 393224 | tf_op jit(solution)/shard_map/ppermute | solution.py:460
  41.1 9.7 %collective-permute-start.6 = (f32[2,64,256]{2,1,0:T(8,128)S(1)}, f32[2,64,256]{2,1,0:T(8,128)S(1)}, u32[]{:S(2)}, u32[]{:S(2)}) collective-permute-start(f32[2,64,256]{2,1,0:T(8,128)S(1)} %get-tuple-element.40), channel_id=1, source_target_pairs={{0,24},{4,28},{8,16},{12,20},{16,8},{20,12},{24,0},{28,4},{1,25},{... | collective-permute-start | bytes 393224 | tf_op jit(solution)/shard_map/ppermute | solution.py:460
  43.6 12.0 %collective-permute-start.7 = (f32[2,64,256]{2,1,0:T(8,128)S(1)}, f32[2,64,256]{2,1,0:T(8,128)S(1)}, u32[]{:S(2)}, u32[]{:S(2)}) collective-permute-start(f32[2,64,256]{2,1,0:T(8,128)S(1)} %get-tuple-element.41), channel_id=1, source_target_pairs={{0,16},{4,20},{8,24},{12,28},{16,0},{20,4},{24,8},{28,12},{1,17},{... | collective-permute-start | bytes 393224 | tf_op jit(solution)/shard_map/ppermute | solution.py:460
  46.6 9.0 %collective-permute-start.5 = (f32[4,48,256]{2,1,0:T(8,128)S(1)}, f32[4,48,256]{2,1,0:T(8,128)S(1)}, u32[]{:S(2)}, u32[]{:S(2)}) collective-permute-start(f32[4,48,256]{2,1,0:T(8,128)S(1)} %slice.141), channel_id=1, source_target_pairs={{0,2},{1,3},{2,0},{3,1},{4,6},{5,7},{6,4},{7,5},{8,10},{9,11},{10,... | collective-permute-start | bytes 589832 | tf_op jit(solution)/shard_map/ppermute | solution.py:460
  49.1 8.1 %collective-permute-start.10 = (f32[4,48,256]{2,1,0:T(8,128)S(1)}, f32[4,48,256]{2,1,0:T(8,128)S(1)}, u32[]{:S(2)}, u32[]{:S(2)}) collective-permute-start(f32[4,48,256]{2,1,0:T(8,128)S(1)} %slice_add_fusion.4), channel_id=1, source_target_pairs={{0,4},{4,0},{8,12},{12,8},{16,20},{20,16},{24,28},{28,24},{1,5},{5... | collective-permute-start | bytes 589832 | tf_op jit(solution)/shard_map/ppermute | solution.py:460
  55.6 6.2 %collective-permute-start.14 = (f32[64,256]{1,0:T(8,128)S(1)}, f32[64,256]{1,0:T(8,128)S(1)}, u32[]{:S(2)}, u32[]{:S(2)}) collective-permute-start(f32[64,256]{1,0:T(8,128)S(1)} %slice_bitcast_fusion), channel_id=1, source_target_pairs={{0,4},{4,0},{8,12},{12,8},{16,20},{20,16},{24,28},{28,24},{1,5},{5... | collective-permute-start | bytes 196616 | tf_op jit(solution)/shard_map/ppermute | solution.py:460
  57.3 7.7 %collective-permute-start.11 = (f32[96,256]{1,0:T(8,128)S(1)}, f32[96,256]{1,0:T(8,128)S(1)}, u32[]{:S(2)}, u32[]{:S(2)}) collective-permute-start(f32[96,256]{1,0:T(8,128)S(1)} %get-tuple-element.42), channel_id=1, source_target_pairs={{0,24},{4,28},{8,16},{12,20},{16,8},{20,12},{24,0},{28,4},{1,25},{... | collective-permute-start | bytes 294920 | tf_op jit(solution)/shard_map/ppermute | solution.py:460
  60.1 6.9 %collective-permute-start.13 = (f32[96,256]{1,0:T(8,128)S(1)}, f32[96,256]{1,0:T(8,128)S(1)}, u32[]{:S(2)}, u32[]{:S(2)}) collective-permute-start(f32[96,256]{1,0:T(8,128)S(1)} %get-tuple-element.43), channel_id=1, source_target_pairs={{0,8},{4,12},{8,0},{12,4},{16,24},{20,28},{24,16},{28,20},{1,9},{5... | collective-permute-start | bytes 294920 | tf_op jit(solution)/shard_map/ppermute | solution.py:460
  60.1 7.7 %collective-permute-start.12 = (f32[96,256]{1,0:T(8,128)S(1)}, f32[96,256]{1,0:T(8,128)S(1)}, u32[]{:S(2)}, u32[]{:S(2)}) collective-permute-start(f32[96,256]{1,0:T(8,128)S(1)} %get-tuple-element.44), channel_id=1, source_target_pairs={{0,16},{4,20},{8,24},{12,28},{16,0},{20,4},{24,8},{28,12},{1,17},{... | collective-permute-start | bytes 294920 | tf_op jit(solution)/shard_map/ppermute | solution.py:460
  67.8 5.4 %collective-permute-start.15 = (f32[160,256]{1,0:T(8,128)S(1)}, f32[160,256]{1,0:T(8,128)S(1)}, u32[]{:S(2)}, u32[]{:S(2)}) collective-permute-start(f32[160,256]{1,0:T(8,128)S(1)} %pad_maximum_fusion.2), channel_id=1, source_target_pairs={{0,2},{1,3},{2,0},{3,1},{4,6},{5,7},{6,4},{7,5},{8,10},{9,11},{10,... | collective-permute-start | bytes 491528 | tf_op jit(solution)/shard_map/ppermute | solution.py:460
  73.2 1.6 %collective-permute-start.16 = (f32[256,256]{1,0:T(8,128)S(1)}, f32[256,256]{1,0:T(8,128)S(1)}, u32[]{:S(2)}, u32[]{:S(2)}) collective-permute-start(f32[256,256]{1,0:T(8,128)S(1)} %pad_maximum_fusion.1.mine), channel_id=1, source_target_pairs={{0,1},{1,0},{2,3},{3,2},{4,5},{5,4},{6,7},{7,6},{8,9},{9,8},{10,11... | collective-permute-start | bytes 786440 | tf_op jit(solution)/shard_map/ppermute | solution.py:460

commit v2 on v1

--- a/solution.py
+++ b/solution.py
@@ -47,12 +47,10 @@
             pltpu.make_async_copy(mod_hbm.at[c, t], mod.at[c, t], arrived.at[1, c, t]),
         )
 
-    def request(group):
+    for group in range(count):
         for k in range(GROUP):
             for copy in fetch(group, k):
                 copy.start()
-
-    request(0)
 
     def build(group, k, start, sums):
         c, t = place(group, k)
@@ -149,8 +147,6 @@
     for k in range(GROUP):
         for copy in fetch(0, k):
             copy.wait()
-        if k + 1 < count:
-            request(k + 1)
 
         def chunk(index, sums, k=k):
             return build(0, k, pl.multiple_of(index * rows, rows), sums)
@@ -163,8 +159,6 @@
             for k in range(GROUP):
                 for copy in fetch(group + 1, k):
                     copy.wait()
-            if group + 1 + GROUP < count:
-                request(group + 1 + GROUP)
             later = build_in_pieces(group + 1)
         share = -(-(N // rows) // (ITERS - 1))
 
@@ -229,7 +223,7 @@
     send, keep = refs[:2]
     own_cells, refs = refs[2 : 2 + CELLS], refs[2 + CELLS :]
     cells, refs = refs[:CELLS], refs[CELLS:]
-    vis, inverse, down_even, down_odd, arrived = refs[:5]
+    vis, down_lines, along_lines, factors_even, factors_odd, arrived = refs[:6]
     steps = channels * intervals
 
     def fetch(step):
@@ -237,15 +231,19 @@
             vis_hbm.at[step // intervals, step % intervals], vis.at[step], arrived.at[step]
         )
 
-    for step in range(2):
+    for step in range(steps):
         fetch(step).start()
 
-    def spread(at, down):
-        for part in range(2):
-            for i in range(GROUPS):
-                span = slice(i * BLK, (i + 1) * BLK)
-                down[part, span, :] = jnp.broadcast_to(inverse[at, part : part + 1, span], (BLK, BLK)).T
-
+    def factor(at, factors, i):
+        span = slice(i * (N // 2), (i + 1) * (N // 2))
+        factors[span, :] = jnp.dot(
+            down_lines[at, :, span].T.astype(jnp.bfloat16),
+            along_lines[at].astype(jnp.bfloat16),
+            preferred_element_type=jnp.float32,
+        )
+
+    down_lines[...] = jnp.zeros_like(down_lines)
+    along_lines[...] = jnp.zeros_like(along_lines)
     for channel in range(channels):
         width = width_ref[channel]
         for interval in range(intervals):
@@ -265,46 +263,52 @@
                 count = count + inside
             smooth = smooth / count
             squares = smooth * smooth
-            denominator = jnp.maximum(squares[0:1] + squares[1:2], 1.0)
+            inverse = smooth / jnp.maximum(squares[0:1] + squares[1:2], 1.0)
+            high = inverse.astype(jnp.bfloat16).astype(jnp.float32)
+            low = inverse - high
+            re_high, im_high = high[0:1], -high[1:2]
+            re_low, im_low = low[0:1], -low[1:2]
             at = channel * intervals + interval
-            inverse[at, 0:1, :] = smooth[0:1] / denominator
-            inverse[at, 1:2, :] = -smooth[1:2] / denominator
+            down = (re_high, re_high, re_low, im_high, im_high, im_low)
+            along_re = (re_high, re_low, re_high, im_high, im_low, im_high)
+            along_im = (-im_high, -im_low, -im_high, re_high, re_low, re_high)
+            for k in range(6):
+                down_lines[at, k : k + 1, :] = down[k]
+                along_lines[at, k : k + 1, :N] = along_re[k]
+                along_lines[at, k : k + 1, N:] = along_im[k]
+    for i in range(2):
+        factor(0, factors_even, i)
+
     for array in cells:
         array[...] = jnp.zeros_like(array)
-    spread(0, down_even)
 
     def add_later(waiting):
         cell, piece, value_re, value_im = waiting
         cells[piece][cell] += value_re
         cells[PIECES + piece][cell] += value_im
 
-    def calibrate(step, down, next_down):
+    def calibrate(step, factors, next_factors):
         channel = step // intervals
         interval = step % intervals
-        spread(jnp.minimum(step + 1, steps - 1), next_down)
         waiting = []
         for i in range(GROUPS):
-            cell = [
-                weight_ref[channel, block] * BANKS + target_ref[channel, interval * GROUPS * GROUPS + block]
-                for block in range(i * GROUPS, (i + 1) * GROUPS)
-            ]
+            if i % 2 == 0:
+                factor(jnp.minimum(step + 1, steps - 1), next_factors, i // 2)
             for j in range(GROUPS):
+                block = i * GROUPS + j
+                cell = weight_ref[channel, block] * BANKS + target_ref[channel, interval * GROUPS * GROUPS + block]
                 span = slice(j * BLK, (j + 1) * BLK)
                 for piece in range(PIECES):
                     at = slice(i * BLK + piece * PIECE, i * BLK + (piece + 1) * PIECE)
-                    row_re = down[0, at, :]
-                    row_im = down[1, at, :]
                     vis_re = vis[step, 0, at, span].astype(jnp.float32)
                     vis_im = vis[step, 1, at, span].astype(jnp.float32)
-                    col_re = inverse[step, 0:1, span]
-                    col_im = inverse[step, 1:2, span]
-                    left_re = row_re * vis_re - row_im * vis_im
-                    left_im = row_re * vis_im + row_im * vis_re
-                    out_re = left_re * col_re + left_im * col_im
-                    out_im = left_im * col_re - left_re * col_im
+                    fac_re = factors[at, span]
+                    fac_im = factors[at, N + j * BLK : N + (j + 1) * BLK]
+                    out_re = fac_re * vis_re - fac_im * vis_im
+                    out_im = fac_re * vis_im + fac_im * vis_re
                     if len(waiting) == 2:
                         add_later(waiting.pop(0))
-                    waiting.append((cell[j], piece, out_re, out_im))
+                    waiting.append((cell, piece, out_re, out_im))
         for entry in waiting:
             add_later(entry)
 
@@ -312,12 +316,10 @@
         step = 2 * turn
         fetch(step).wait()
         fetch(step + 1).wait()
-        calibrate(step, down_even, down_odd)
-        calibrate(step + 1, down_odd, down_even)
+        calibrate(step, factors_even, factors_odd)
+        calibrate(step + 1, factors_odd, factors_even)
         return carry
 
-    for step in range(2, steps):
-        fetch(step).start()
     lax.fori_loop(0, steps // 2, pair, 0)
     four = BANKS // 2
 
@@ -327,7 +329,7 @@
             out[w * four + turn] = array[own]
         return w * BANKS + place_ref[3 + turn]
 
-    bank_products(place_ref, cells, cell_of, left_ref, table, send, keep, *refs[5:])
+    bank_products(place_ref, cells, cell_of, left_ref, table, send, keep, *refs[6:])
 
 
 def own_products_kernel(place_ref, left_ref, table, *refs):
@@ -420,9 +422,10 @@
         scratch_shapes=[pltpu.VMEM((NWEIGHT * BANKS, PIECE, BLK), jnp.float32)] * CELLS
         + [
             pltpu.VMEM((steps, 2, N, N), jnp.bfloat16),
-            pltpu.VMEM((steps, 8, N), jnp.float32),
-            pltpu.VMEM((2, N, BLK), jnp.float32),
-            pltpu.VMEM((2, N, BLK), jnp.float32),
+            pltpu.VMEM((steps, 16, N), jnp.float32),
+            pltpu.VMEM((steps, 16, 2 * N), jnp.float32),
+            pltpu.VMEM((N, 2 * N), jnp.float32),
+            pltpu.VMEM((N, 2 * N), jnp.float32),
             pltpu.SemaphoreType.DMA((steps,)),
         ]
         + product_scratch,
@@ -460,32 +463,18 @@
     return lax.ppermute(value, axis, [(i, i ^ mask) for i in range(count)])
 
 
-def assemble_kernel(place_ref, mine, other, out, done):
+def assemble_kernel(place_ref, mine, other, out):
     core = place_ref[1]
     across = place_ref[2]
     half_p, half_q = ROWS[0] // 2, ROWS[1] // 2
-    copies = []
     for part, rows in ((core, mine), (1 - core, other)):
         base = part * BEAMS
-        pieces = [
-            (at + half * size, size)
-            for half in (across, 1 - across)
-            for at, size in ((0, half_p), (ROWS[0], half_q))
-        ] + [(ROWS[0] + ROWS[1], ROWS[2])]
         start = 0
-        for at, size in pieces:
-            copies.append(
-                pltpu.make_async_copy(
-                    rows.at[start : start + size],
-                    out.at[pl.ds(pl.multiple_of(base + at, 16), size)],
-                    done.at[len(copies)],
-                )
-            )
-            start += size
-    for copy in copies:
-        copy.start()
-    for copy in copies:
-        copy.wait()
+        for half in (across, 1 - across):
+            for at, size in ((0, half_p), (ROWS[0], half_q)):
+                out[pl.ds(pl.multiple_of(base + at + half * size, 16), size), :] = rows[start : start + size, :]
+                start += size
+        out[pl.ds(pl.multiple_of(base + start, 16), ROWS[2]), :] = rows[start:, :]
 
 
 def reduce_banks(place, send_away, keep_away, send_own, keep_own):
@@ -518,17 +507,17 @@
     r_here = r_here[0] + swap(r_here[1], "chan", 1)
     here = jnp.concatenate([p_here, q_here], axis=1)
     z_got = [swap(here[k], "chan", 2 * k) for k in (3, 2, 1)]
+    r_got = swap(r_here, "tm", 2)
+    r_got, *z_got = lax.optimization_barrier((r_got, *z_got))
     here = here[0] + z_got[0] + z_got[1] + z_got[2]
-    x_got = swap(jnp.concatenate([here, r_here], axis=0), "tm", 2)
-    pq = half_p + half_q
-    mine = jnp.concatenate([here, x_got[:pq], r_here + x_got[pq:]], axis=0)
+    r_here = r_here + r_got
+    mine = jnp.concatenate([here, swap(here, "tm", 2), r_here], axis=0)
     other = swap(mine, "tm", 1)
     return pl.pallas_call(
         assemble_kernel,
         in_specs=[SCALARS, VECTORS, VECTORS],
-        out_specs=pl.BlockSpec(memory_space=pltpu.HBM),
+        out_specs=VECTORS,
         out_shape=jax.ShapeDtypeStruct((2 * BEAMS, BEAMS), jnp.float32),
-        scratch_shapes=[pltpu.SemaphoreType.DMA((10,))],
         compiler_params=pltpu.CompilerParams(vmem_limit_bytes=PREPARE_VMEM),
         name="assemble",
     )(place, mine, other)

time: 76.6 us -> 77.3 us (level)
    pallas_call x1, Pallas kernels: 10.6 us -> 11.7 us  [beam_products(): pl.pallas_call(functools.partial(calibrate_kernel, channels=channels, int...]
    ppermute x15 -> x16, waiting for transfers between devices: 21.1 us -> 21.8 us  [swap(): return lax.ppermute(value, axis, [(i, i ^ mask) for i in range(count)])]
    ppermute x15 -> x16, starting transfers between devices: 18.7 us -> 18.3 us  [swap(): return lax.ppermute(value, axis, [(i, i ^ mask) for i in range(count)])]
  transfers between devices with their start and end apart: 17 -> 18, of which waited for: 11 -> 10; matrix products, arithmetic and copies ran while one was open for 1% -> 1% of each run, Pallas kernels for 5% -> 5%
where the time goes in v2:
time: 77.3 us; the launch traced here: 77.1 us
  Pallas kernels  30.4 us (39%)
  starting transfers between devices  23.5 us (30%)
  waiting for transfers between devices  22.2 us (29%)
    ppermute x16, waiting for transfers between devices, swap(): return lax.ppermute(value, axis, [(i, i ^ mask) for i in range(count)])  21.8 us
    ppermute x16, starting transfers between devices, swap(): return lax.ppermute(value, axis, [(i, i ^ mask) for i in range(count)])  18.3 us
    pallas_call x1, Pallas kernels, referenced_gains(): pl.pallas_call(functools.partial(gains_kernel, channels=channels, interva...  13.7 us
    pallas_call x1, Pallas kernels, beam_products(): pl.pallas_call(functools.partial(calibrate_kernel, channels=channels, int...  11.7 us
    ppermute x1, starting transfers between devices, neighbour_gains(): lax.ppermute(jnp.where(odd, head, tail), 'tm', [(i, i ^ 1) for i in range...  4.38 us
    pallas_call x1, Pallas kernels, beam_products(): pl.pallas_call(own_products_kernel, in_specs=[SCALARS] + [VECTORS] * (2 +...  3.45 us
  transfers between devices with their start and end apart: 18, of which 10 were waited for; matrix products, arithmetic and copies ran while one was open for 1% of the time, Pallas kernels for 5%

profile of v2, /device:TPU:0, one launch (start us, length us, event | category | flops | bytes accessed | tf_op | source)
XLA Modules:
  0.0 77.1 jit_solution(9557200726749708053)
XLA Ops:
  0.0 13.7 %gains.1.mid_ref = f32[2,4,2,512]{3,2,1,0:T(2,128)S(1)} custom-call(bf16[2,4,2,512,512]{4,3,2,1,0:T(8,128)(2,1)} %vis_hbm.3, bf16[2,4,2,512,512]{4,3,2,1,0:T(8,128)(2,1)} %mod_hbm.1), custom_call_target="tpu_custom_call" | custom-call | flops 125829120 | bytes 16777216 | tf_op jit(solution)/shard_map/gains/pallas_call | solution.py:183
  13.8 0.8 %collective-permute-start.1 = (f32[2,2,2,512]{3,2,1,0:T(2,128)S(1)}, f32[2,2,2,512]{3,2,1,0:T(2,128)S(1)}, u32[]{:S(2)}, u32[]{:S(2)}) collective-permute-start(f32[2,2,2,512]{3,2,1,0:T(2,128)S(1)} %get-tuple-element.55), channel_id=1, source_target_pairs={{1,2},{2,1},{5,6},{6,5},{9,10},{10,9},{13,14},{14,13},{17,18},{18,... | collective-permute-start | bytes 49160 | tf_op jit(solution)/shard_map/ppermute | solution.py:541
  14.6 4.4 %collective-permute-start = (f32[2,2,2,512]{3,2,1,0:T(2,128)S(1)}, f32[2,2,2,512]{3,2,1,0:T(2,128)S(1)}, u32[]{:S(2)}, u32[]{:S(2)}) collective-permute-start(f32[2,2,2,512]{3,2,1,0:T(2,128)S(1)} %get-tuple-element.56), channel_id=1, source_target_pairs={{0,1},{1,0},{2,3},{3,2},{4,5},{5,4},{6,7},{7,6},{8,9},{9,8},{10,11... | collective-permute-start | bytes 49160 | tf_op jit(solution)/shard_map/ppermute | solution.py:539
  19.1 0.1 stack.56.place_ref
  19.2 0.2 prepare.1.table
  19.4 0.4 collective-permute-done
  19.9 11.7 %calibrate.1 = (f32[4,256,256]{2,1,0:T(8,128)S(1)}, f32[4,256,256]{2,1,0:T(8,128)S(1)}, f32[32,32,128]{2,1,0:T(8,128)S(1)}, f32[32,32,128]{2,1,0:T(8,128)S(1)}, ...) custom-call(s32[2,16]{1,0:T(2,128)S(1)} %copy-done.2, ...), custom_call_target="tpu_custom_call" | custom-call | flops 2000000000 | bytes 16777216 | tf_op jit(solution)/shard_map/calibrate/pallas_call | solution.py:416
  31.6 0.4 collective-permute-start.3
  32.0 3.4 %products.1 = (f32[4,256,256]{2,1,0:T(8,128)S(1)}, f32[4,256,256]{2,1,0:T(8,128)S(1)}) custom-call(s32[11]{0:T(128)S(1)} %stack.56.place_ref, bf16[8,256,128]{2,1,0:T(8,128)(2,1)S(1)} %copy-done, bf16[1024,256]{1,0:T(8,128)(2,1)S(1)} %prepare.1.table, f32[32,32,128]{2,1,0:T(8,128)S(1)} %get-tuple-element.27.refs_0_, ...), custom_call_target="tpu_custom_call" | custom-call | flops 2000000000 | bytes 2097152 | tf_op jit(solution)/shard_map/products/pallas_call | solution.py:443
  35.4 0.2 collective-permute-start.2
  35.7 1.6 %collective-permute-start.4 = (f32[4,96,256]{2,1,0:T(8,128)S(1)}, f32[4,96,256]{2,1,0:T(8,128)S(1)}, u32[]{:S(2)}, u32[]{:S(2)}) collective-permute-start(f32[4,96,256]{2,1,0:T(8,128)S(1)} %slice_add_fusion), channel_id=1, source_target_pairs={{0,4},{4,0},{8,12},{12,8},{16,20},{20,16},{24,28},{28,24},{1,5},{5... | collective-permute-start | bytes 1179656 | tf_op jit(solution)/shard_map/ppermute | solution.py:463
  37.3 0.8 %collective-permute-done.2 = f32[4,256,256]{2,1,0:T(8,128)S(1)} collective-permute-done((f32[4,256,256]{2,1,0:T(8,128)S(1)}, f32[4,256,256]{2,1,0:T(8,128)S(1)}, u32[]{:S(2)}, u32[]{:S(2)}) %collective-permute-start.2) | collective-permute-done | bytes 1048608 | tf_op jit(solution)/shard_map/ppermute | solution.py:463
  38.2 1.8 %collective-permute-start.9 = (f32[8,48,256]{2,1,0:T(8,128)S(1)}, f32[8,48,256]{2,1,0:T(8,128)S(1)}, u32[]{:S(2)}, u32[]{:S(2)}) collective-permute-start(f32[8,48,256]{2,1,0:T(8,128)S(1)} %pad_maximum_fusion), channel_id=1, source_target_pairs={{0,2},{1,3},{2,0},{3,1},{4,6},{5,7},{6,4},{7,5},{8,10},{9,11},{10,... | collective-permute-start | bytes 1179656 | tf_op jit(solution)/shard_map/ppermute | solution.py:463
  40.2 1.6 %collective-permute-start.8 = (f32[2,64,256]{2,1,0:T(8,128)S(1)}, f32[2,64,256]{2,1,0:T(8,128)S(1)}, u32[]{:S(2)}, u32[]{:S(2)}) collective-permute-start(f32[2,64,256]{2,1,0:T(8,128)S(1)} %get-tuple-element.47), channel_id=1, source_target_pairs={{0,8},{4,12},{8,0},{12,4},{16,24},{20,28},{24,16},{28,20},{1,9},{5... | collective-permute-start | bytes 393224 | tf_op jit(solution)/shard_map/ppermute | solution.py:463
  41.8 2.5 %collective-permute-start.6 = (f32[2,64,256]{2,1,0:T(8,128)S(1)}, f32[2,64,256]{2,1,0:T(8,128)S(1)}, u32[]{:S(2)}, u32[]{:S(2)}) collective-permute-start(f32[2,64,256]{2,1,0:T(8,128)S(1)} %get-tuple-element.48), channel_id=1, source_target_pairs={{0,24},{4,28},{8,16},{12,20},{16,8},{20,12},{24,0},{28,4},{1,25},{... | collective-permute-start | bytes 393224 | tf_op jit(solution)/shard_map/ppermute | solution.py:463
  44.3 0.1 collective-permute-start.7
  44.4 2.8 %collective-permute-done.4 = f32[4,96,256]{2,1,0:T(8,128)S(1)} collective-permute-done((f32[4,96,256]{2,1,0:T(8,128)S(1)}, f32[4,96,256]{2,1,0:T(8,128)S(1)}, u32[]{:S(2)}, u32[]{:S(2)}) %collective-permute-start.4) | collective-permute-done | bytes 393248 | tf_op jit(solution)/shard_map/ppermute | solution.py:463
  47.3 1.7 %collective-permute-start.5 = (f32[4,48,256]{2,1,0:T(8,128)S(1)}, f32[4,48,256]{2,1,0:T(8,128)S(1)}, u32[]{:S(2)}, u32[]{:S(2)}) collective-permute-start(f32[4,48,256]{2,1,0:T(8,128)S(1)} %slice.133), channel_id=1, source_target_pairs={{0,2},{1,3},{2,0},{3,1},{4,6},{5,7},{6,4},{7,5},{8,10},{9,11},{10,... | collective-permute-start | bytes 589832 | tf_op jit(solution)/shard_map/ppermute | solution.py:463
  49.0 0.9 %collective-permute-done.9 = f32[8,48,256]{2,1,0:T(8,128)S(1)} collective-permute-done((f32[8,48,256]{2,1,0:T(8,128)S(1)}, f32[8,48,256]{2,1,0:T(8,128)S(1)}, u32[]{:S(2)}, u32[]{:S(2)}) %collective-permute-start.9) | collective-permute-done | bytes 393248 | tf_op jit(solution)/shard_map/ppermute | solution.py:463
  49.9 1.6 %collective-permute-start.10 = (f32[4,48,256]{2,1,0:T(8,128)S(1)}, f32[4,48,256]{2,1,0:T(8,128)S(1)}, u32[]{:S(2)}, u32[]{:S(2)}) collective-permute-start(f32[4,48,256]{2,1,0:T(8,128)S(1)} %slice_add_fusion.4), channel_id=1, source_target_pairs={{0,4},{4,0},{8,12},{12,8},{16,20},{20,16},{24,28},{28,24},{1,5},{5... | collective-permute-start | bytes 589832 | tf_op jit(solution)/shard_map/ppermute | solution.py:463
  51.5 4.8 %collective-permute-done.7 = f32[2,64,256]{2,1,0:T(8,128)S(1)} collective-permute-done((f32[2,64,256]{2,1,0:T(8,128)S(1)}, f32[2,64,256]{2,1,0:T(8,128)S(1)}, u32[]{:S(2)}, u32[]{:S(2)}) %collective-permute-start.7) | collective-permute-done | bytes 131104 | tf_op jit(solution)/shard_map/ppermute | solution.py:463
  56.3 1.6 %collective-permute-start.11 = (f32[64,256]{1,0:T(8,128)S(1)}, f32[64,256]{1,0:T(8,128)S(1)}, u32[]{:S(2)}, u32[]{:S(2)}) collective-permute-start(f32[64,256]{1,0:T(8,128)S(1)} %slice_bitcast_fusion), channel_id=1, source_target_pairs={{0,4},{4,0},{8,12},{12,8},{16,20},{20,16},{24,28},{28,24},{1,5},{5... | collective-permute-start | bytes 196616 | tf_op jit(solution)/shard_map/ppermute | solution.py:463
  58.1 2.9 %collective-permute-start.13 = (f32[96,256]{1,0:T(8,128)S(1)}, f32[96,256]{1,0:T(8,128)S(1)}, u32[]{:S(2)}, u32[]{:S(2)}) collective-permute-start(f32[96,256]{1,0:T(8,128)S(1)} %get-tuple-element.51), channel_id=1, source_target_pairs={{0,24},{4,28},{8,16},{12,20},{16,8},{20,12},{24,0},{28,4},{1,25},{... | collective-permute-start | bytes 294920 | tf_op jit(solution)/shard_map/ppermute | solution.py:463
  61.0 0.6 collective-permute-start.14
  61.6 1.1 %collective-permute-start.12 = (f32[64,256]{1,0:T(8,128)S(1)}, f32[64,256]{1,0:T(8,128)S(1)}, u32[]{:S(2)}, u32[]{:S(2)}) collective-permute-start(f32[64,256]{1,0:T(8,128)S(1)} %fusion.24), channel_id=1, source_target_pairs={{0,2},{1,3},{2,0},{3,1},{4,6},{5,7},{6,4},{7,5},{8,10},{9,11},{10,... | collective-permute-start | bytes 196616 | tf_op jit(solution)/shard_map/ppermute | solution.py:463
  62.7 1.3 %collective-permute-done.15 = f32[96,256]{1,0:T(8,128)S(1)} collective-permute-done((f32[96,256]{1,0:T(8,128)S(1)}, f32[96,256]{1,0:T(8,128)S(1)}, u32[]{:S(2)}, u32[]{:S(2)}) %collective-permute-start.15) | collective-permute-done | bytes 98336 | tf_op jit(solution)/shard_map/ppermute | solution.py:463
  64.1 1.9 %collective-permute-done.13 = f32[96,256]{1,0:T(8,128)S(1)} collective-permute-done((f32[96,256]{1,0:T(8,128)S(1)}, f32[96,256]{1,0:T(8,128)S(1)}, u32[]{:S(2)}, u32[]{:S(2)}) %collective-permute-start.13) | collective-permute-done | bytes 98336 | tf_op jit(solution)/shard_map/ppermute | solution.py:463
  65.9 3.5 %collective-permute-done.14 = f32[96,256]{1,0:T(8,128)S(1)} collective-permute-done((f32[96,256]{1,0:T(8,128)S(1)}, f32[96,256]{1,0:T(8,128)S(1)}, u32[]{:S(2)}, u32[]{:S(2)}) %collective-permute-start.14) | collective-permute-done | bytes 98336 | tf_op jit(solution)/shard_map/ppermute | solution.py:463
  69.5 0.4 collective-permute-start.16
  69.9 4.3 %collective-permute-done.16 = f32[96,256]{1,0:T(8,128)S(1)} collective-permute-done((f32[96,256]{1,0:T(8,128)S(1)}, f32[96,256]{1,0:T(8,128)S(1)}, u32[]{:S(2)}, u32[]{:S(2)}) %collective-permute-start.16) | collective-permute-done | bytes 98336 | tf_op jit(solution)/shard_map/ppermute | solution.py:463
  74.2 1.5 %collective-permute-done.17.other = f32[256,256]{1,0:T(8,128)S(1)} collective-permute-done((f32[256,256]{1,0:T(8,128)S(1)}, f32[256,256]{1,0:T(8,128)S(1)}, u32[]{:S(2)}, u32[]{:S(2)}) %collective-permute-start.17) | collective-permute-done | bytes 262176 | tf_op jit(solution)/shard_map/ppermute | solution.py:463
  75.8 1.4 %assemble.1 = f32[512,256]{1,0:T(8,128)} custom-call(s32[11]{0:T(128)S(1)} %stack.56.place_ref, f32[256,256]{1,0:T(8,128)S(1)} %pad_maximum_fusion.1.mine, f32[256,256]{1,0:T(8,128)S(1)} %collective-permute-done.17.other), custom_call_target="tpu_custom_call" | custom-call | tf_op jit(solution)/shard_map/assemble/pallas_call | solution.py:516
  (42 shorter events, 0.9 us)
Async XLA Ops:
  0.0 19.0 %copy-start.4 = (s32[2,4,16]{2,1,0:T(4,128)S(1)}, s32[2,4,16]{2,1,0:T(4,128)}, u32[]{:S(2)}) copy-start(s32[2,4,16]{2,1,0:T(4,128)} %param.12) | copy-start | bytes 1540
  0.0 19.2 %copy-start.1 = (bf16[8,256,128]{2,1,0:T(8,128)(2,1)S(1)}, bf16[8,256,128]{2,1,0:T(8,128)(2,1)}, u32[]{:S(2)}) copy-start(bf16[8,256,128]{2,1,0:T(8,128)(2,1)} %right_ref) | copy-start | bytes 1572868
  0.0 19.9 %copy-start = (bf16[8,256,128]{2,1,0:T(8,128)(2,1)S(1)}, bf16[8,256,128]{2,1,0:T(8,128)(2,1)}, u32[]{:S(2)}) copy-start(bf16[8,256,128]{2,1,0:T(8,128)(2,1)} %left_ref.3) | copy-start | bytes 1572868
  0.0 19.9 %copy-start.2 = (s32[2,16]{1,0:T(2,128)S(1)}, s32[2,16]{1,0:T(2,128)}, u32[]{:S(2)}) copy-start(s32[2,16]{1,0:T(2,128)} %weight_ref.1) | copy-start | bytes 388
  0.0 19.9 %copy-start.3 = (s32[2]{0:T(128)S(1)}, s32[2]{0:T(128)}, u32[]{:S(2)}) copy-start(s32[2]{0:T(128)} %width_ref.1) | copy-start | bytes 28
  13.8 5.6 %collective-permute-start.1 = (f32[2,2,2,512]{3,2,1,0:T(2,128)S(1)}, f32[2,2,2,512]{3,2,1,0:T(2,128)S(1)}, u32[]{:S(2)}, u32[]{:S(2)}) collective-permute-start(f32[2,2,2,512]{3,2,1,0:T(2,128)S(1)} %get-tuple-element.55), channel_id=1, source_target_pairs={{1,2},{2,1},{5,6},{6,5},{9,10},{10,9},{13,14},{14,13},{17,18},{18,... | collective-permute-start | bytes 49160 | tf_op jit(solution)/shard_map/ppermute | solution.py:541
  14.6 5.2 %collective-permute-start = (f32[2,2,2,512]{3,2,1,0:T(2,128)S(1)}, f32[2,2,2,512]{3,2,1,0:T(2,128)S(1)}, u32[]{:S(2)}, u32[]{:S(2)}) collective-permute-start(f32[2,2,2,512]{3,2,1,0:T(2,128)S(1)} %get-tuple-element.56), channel_id=1, source_target_pairs={{0,1},{1,0},{2,3},{3,2},{4,5},{5,4},{6,7},{7,6},{8,9},{9,8},{10,11... | collective-permute-start | bytes 49160 | tf_op jit(solution)/shard_map/ppermute | solution.py:539
  31.6 4.1 %collective-permute-start.3 = (f32[4,256,256]{2,1,0:T(8,128)S(1)}, f32[4,256,256]{2,1,0:T(8,128)S(1)}, u32[]{:S(2)}, u32[]{:S(2)}) collective-permute-start(f32[4,256,256]{2,1,0:T(8,128)S(1)} %get-tuple-element.38), channel_id=1, source_target_pairs={{0,1},{1,0},{2,3},{3,2},{4,5},{5,4},{6,7},{7,6},{8,9},{9,8},{10,11... | collective-permute-start | bytes 3145736 | tf_op jit(solution)/shard_map/ppermute | solution.py:463
  35.4 2.7 %collective-permute-start.2 = (f32[4,256,256]{2,1,0:T(8,128)S(1)}, f32[4,256,256]{2,1,0:T(8,128)S(1)}, u32[]{:S(2)}, u32[]{:S(2)}) collective-permute-start(f32[4,256,256]{2,1,0:T(8,128)S(1)} %get-tuple-element.36), channel_id=1, source_target_pairs={{0,1},{1,0},{2,3},{3,2},{4,5},{5,4},{6,7},{7,6},{8,9},{9,8},{10,11... | collective-permute-start | bytes 3145736 | tf_op jit(solution)/shard_map/ppermute | solution.py:463
  35.7 11.4 %collective-permute-start.4 = (f32[4,96,256]{2,1,0:T(8,128)S(1)}, f32[4,96,256]{2,1,0:T(8,128)S(1)}, u32[]{:S(2)}, u32[]{:S(2)}) collective-permute-start(f32[4,96,256]{2,1,0:T(8,128)S(1)} %slice_add_fusion), channel_id=1, source_target_pairs={{0,4},{4,0},{8,12},{12,8},{16,20},{20,16},{24,28},{28,24},{1,5},{5... | collective-permute-start | bytes 1179656 | tf_op jit(solution)/shard_map/ppermute | solution.py:463
  38.2 11.6 %collective-permute-start.9 = (f32[8,48,256]{2,1,0:T(8,128)S(1)}, f32[8,48,256]{2,1,0:T(8,128)S(1)}, u32[]{:S(2)}, u32[]{:S(2)}) collective-permute-start(f32[8,48,256]{2,1,0:T(8,128)S(1)} %pad_maximum_fusion), channel_id=1, source_target_pairs={{0,2},{1,3},{2,0},{3,1},{4,6},{5,7},{6,4},{7,5},{8,10},{9,11},{10,... | collective-permute-start | bytes 1179656 | tf_op jit(solution)/shard_map/ppermute | solution.py:463
  40.2 11.3 %collective-permute-start.8 = (f32[2,64,256]{2,1,0:T(8,128)S(1)}, f32[2,64,256]{2,1,0:T(8,128)S(1)}, u32[]{:S(2)}, u32[]{:S(2)}) collective-permute-start(f32[2,64,256]{2,1,0:T(8,128)S(1)} %get-tuple-element.47), channel_id=1, source_target_pairs={{0,8},{4,12},{8,0},{12,4},{16,24},{20,28},{24,16},{28,20},{1,9},{5... | collective-permute-start | bytes 393224 | tf_op jit(solution)/shard_map/ppermute | solution.py:463
  41.8 9.7 %collective-permute-start.6 = (f32[2,64,256]{2,1,0:T(8,128)S(1)}, f32[2,64,256]{2,1,0:T(8,128)S(1)}, u32[]{:S(2)}, u32[]{:S(2)}) collective-permute-start(f32[2,64,256]{2,1,0:T(8,128)S(1)} %get-tuple-element.48), channel_id=1, source_target_pairs={{0,24},{4,28},{8,16},{12,20},{16,8},{20,12},{24,0},{28,4},{1,25},{... | collective-permute-start | bytes 393224 | tf_op jit(solution)/shard_map/ppermute | solution.py:463
  44.3 12.0 %collective-permute-start.7 = (f32[2,64,256]{2,1,0:T(8,128)S(1)}, f32[2,64,256]{2,1,0:T(8,128)S(1)}, u32[]{:S(2)}, u32[]{:S(2)}) collective-permute-start(f32[2,64,256]{2,1,0:T(8,128)S(1)} %get-tuple-element.49), channel_id=1, source_target_pairs={{0,16},{4,20},{8,24},{12,28},{16,0},{20,4},{24,8},{28,12},{1,17},{... | collective-permute-start | bytes 393224 | tf_op jit(solution)/shard_map/ppermute | solution.py:463
  47.3 9.0 %collective-permute-start.5 = (f32[4,48,256]{2,1,0:T(8,128)S(1)}, f32[4,48,256]{2,1,0:T(8,128)S(1)}, u32[]{:S(2)}, u32[]{:S(2)}) collective-permute-start(f32[4,48,256]{2,1,0:T(8,128)S(1)} %slice.133), channel_id=1, source_target_pairs={{0,2},{1,3},{2,0},{3,1},{4,6},{5,7},{6,4},{7,5},{8,10},{9,11},{10,... | collective-permute-start | bytes 589832 | tf_op jit(solution)/shard_map/ppermute | solution.py:463
  49.9 8.1 %collective-permute-start.10 = (f32[4,48,256]{2,1,0:T(8,128)S(1)}, f32[4,48,256]{2,1,0:T(8,128)S(1)}, u32[]{:S(2)}, u32[]{:S(2)}) collective-permute-start(f32[4,48,256]{2,1,0:T(8,128)S(1)} %slice_add_fusion.4), channel_id=1, source_target_pairs={{0,4},{4,0},{8,12},{12,8},{16,20},{20,16},{24,28},{28,24},{1,5},{5... | collective-permute-start | bytes 589832 | tf_op jit(solution)/shard_map/ppermute | solution.py:463
  56.3 5.3 %collective-permute-start.11 = (f32[64,256]{1,0:T(8,128)S(1)}, f32[64,256]{1,0:T(8,128)S(1)}, u32[]{:S(2)}, u32[]{:S(2)}) collective-permute-start(f32[64,256]{1,0:T(8,128)S(1)} %slice_bitcast_fusion), channel_id=1, source_target_pairs={{0,4},{4,0},{8,12},{12,8},{16,20},{20,16},{24,28},{28,24},{1,5},{5... | collective-permute-start | bytes 196616 | tf_op jit(solution)/shard_map/ppermute | solution.py:463
  58.1 6.0 %collective-permute-start.15 = (f32[96,256]{1,0:T(8,128)S(1)}, f32[96,256]{1,0:T(8,128)S(1)}, u32[]{:S(2)}, u32[]{:S(2)}) collective-permute-start(f32[96,256]{1,0:T(8,128)S(1)} %get-tuple-element.50), channel_id=1, source_target_pairs={{0,8},{4,12},{8,0},{12,4},{16,24},{20,28},{24,16},{28,20},{1,9},{5... | collective-permute-start | bytes 294920 | tf_op jit(solution)/shard_map/ppermute | solution.py:463
  58.1 7.8 %collective-permute-start.13 = (f32[96,256]{1,0:T(8,128)S(1)}, f32[96,256]{1,0:T(8,128)S(1)}, u32[]{:S(2)}, u32[]{:S(2)}) collective-permute-start(f32[96,256]{1,0:T(8,128)S(1)} %get-tuple-element.51), channel_id=1, source_target_pairs={{0,24},{4,28},{8,16},{12,20},{16,8},{20,12},{24,0},{28,4},{1,25},{... | collective-permute-start | bytes 294920 | tf_op jit(solution)/shard_map/ppermute | solution.py:463
  61.0 8.4 %collective-permute-start.14 = (f32[96,256]{1,0:T(8,128)S(1)}, f32[96,256]{1,0:T(8,128)S(1)}, u32[]{:S(2)}, u32[]{:S(2)}) collective-permute-start(f32[96,256]{1,0:T(8,128)S(1)} %get-tuple-element.52), channel_id=1, source_target_pairs={{0,16},{4,20},{8,24},{12,28},{16,0},{20,4},{24,8},{28,12},{1,17},{... | collective-permute-start | bytes 294920 | tf_op jit(solution)/shard_map/ppermute | solution.py:463
  61.6 7.8 %collective-permute-start.12 = (f32[64,256]{1,0:T(8,128)S(1)}, f32[64,256]{1,0:T(8,128)S(1)}, u32[]{:S(2)}, u32[]{:S(2)}) collective-permute-start(f32[64,256]{1,0:T(8,128)S(1)} %fusion.24), channel_id=1, source_target_pairs={{0,2},{1,3},{2,0},{3,1},{4,6},{5,7},{6,4},{7,5},{8,10},{9,11},{10,... | collective-permute-start | bytes 196616 | tf_op jit(solution)/shard_map/ppermute | solution.py:463
  69.5 4.7 %collective-permute-start.16 = (f32[96,256]{1,0:T(8,128)S(1)}, f32[96,256]{1,0:T(8,128)S(1)}, u32[]{:S(2)}, u32[]{:S(2)}) collective-permute-start(f32[96,256]{1,0:T(8,128)S(1)} %fusion.20), channel_id=1, source_target_pairs={{0,2},{1,3},{2,0},{3,1},{4,6},{5,7},{6,4},{7,5},{8,10},{9,11},{10,... | collective-permute-start | bytes 294920 | tf_op jit(solution)/shard_map/ppermute | solution.py:463
  74.2 1.6 %collective-permute-start.17 = (f32[256,256]{1,0:T(8,128)S(1)}, f32[256,256]{1,0:T(8,128)S(1)}, u32[]{:S(2)}, u32[]{:S(2)}) collective-permute-start(f32[256,256]{1,0:T(8,128)S(1)} %pad_maximum_fusion.1.mine), channel_id=1, source_target_pairs={{0,1},{1,0},{2,3},{3,2},{4,5},{5,4},{6,7},{7,6},{8,9},{9,8},{10,11... | collective-permute-start | bytes 786440 | tf_op jit(solution)/shard_map/ppermute | solution.py:463

commit v3 on v1

--- a/solution.py
+++ b/solution.py
@@ -47,12 +47,10 @@
             pltpu.make_async_copy(mod_hbm.at[c, t], mod.at[c, t], arrived.at[1, c, t]),
         )
 
-    def request(group):
+    for group in range(count):
         for k in range(GROUP):
             for copy in fetch(group, k):
                 copy.start()
-
-    request(0)
 
     def build(group, k, start, sums):
         c, t = place(group, k)
@@ -149,13 +147,11 @@
     for k in range(GROUP):
         for copy in fetch(0, k):
             copy.wait()
-        if k + 1 < count:
-            request(k + 1)
 
         def chunk(index, sums, k=k):
             return build(0, k, pl.multiple_of(index * rows, rows), sums)
 
-        first_gains(0, k, lax.fori_loop(0, N // rows, chunk, (zero, zero, zero), unroll=2))
+        first_gains(0, k, lax.fori_loop(0, N // rows, chunk, (zero, zero, zero), unroll=4))
 
     for group in range(count):
         later = iter(())
@@ -163,8 +159,6 @@
             for k in range(GROUP):
                 for copy in fetch(group + 1, k):
                     copy.wait()
-            if group + 1 + GROUP < count:
-                request(group + 1 + GROUP)
             later = build_in_pieces(group + 1)
         share = -(-(N // rows) // (ITERS - 1))
 
@@ -237,7 +231,7 @@
             vis_hbm.at[step // intervals, step % intervals], vis.at[step], arrived.at[step]
         )
 
-    for step in range(2):
+    for step in range(steps):
         fetch(step).start()
 
     def spread(at, down):
@@ -302,7 +296,7 @@
                     left_im = row_re * vis_im + row_im * vis_re
                     out_re = left_re * col_re + left_im * col_im
                     out_im = left_im * col_re - left_re * col_im
-                    if len(waiting) == 2:
+                    if len(waiting) == 3:
                         add_later(waiting.pop(0))
                     waiting.append((cell[j], piece, out_re, out_im))
         for entry in waiting:
@@ -316,8 +310,6 @@
         calibrate(step + 1, down_odd, down_even)
         return carry
 
-    for step in range(2, steps):
-        fetch(step).start()
     lax.fori_loop(0, steps // 2, pair, 0)
     four = BANKS // 2
 
@@ -460,32 +452,18 @@
     return lax.ppermute(value, axis, [(i, i ^ mask) for i in range(count)])
 
 
-def assemble_kernel(place_ref, mine, other, out, done):
+def assemble_kernel(place_ref, mine, other, out):
     core = place_ref[1]
     across = place_ref[2]
     half_p, half_q = ROWS[0] // 2, ROWS[1] // 2
-    copies = []
     for part, rows in ((core, mine), (1 - core, other)):
         base = part * BEAMS
-        pieces = [
-            (at + half * size, size)
-            for half in (across, 1 - across)
-            for at, size in ((0, half_p), (ROWS[0], half_q))
-        ] + [(ROWS[0] + ROWS[1], ROWS[2])]
         start = 0
-        for at, size in pieces:
-            copies.append(
-                pltpu.make_async_copy(
-                    rows.at[start : start + size],
-                    out.at[pl.ds(pl.multiple_of(base + at, 16), size)],
-                    done.at[len(copies)],
-                )
-            )
-            start += size
-    for copy in copies:
-        copy.start()
-    for copy in copies:
-        copy.wait()
+        for half in (across, 1 - across):
+            for at, size in ((0, half_p), (ROWS[0], half_q)):
+                out[pl.ds(pl.multiple_of(base + at + half * size, 16), size), :] = rows[start : start + size, :]
+                start += size
+        out[pl.ds(pl.multiple_of(base + start, 16), ROWS[2]), :] = rows[start:, :]
 
 
 def reduce_banks(place, send_away, keep_away, send_own, keep_own):
@@ -519,16 +497,14 @@
     here = jnp.concatenate([p_here, q_here], axis=1)
     z_got = [swap(here[k], "chan", 2 * k) for k in (3, 2, 1)]
     here = here[0] + z_got[0] + z_got[1] + z_got[2]
-    x_got = swap(jnp.concatenate([here, r_here], axis=0), "tm", 2)
-    pq = half_p + half_q
-    mine = jnp.concatenate([here, x_got[:pq], r_here + x_got[pq:]], axis=0)
+    r_here = r_here + swap(r_here, "tm", 2)
+    mine = jnp.concatenate([here, swap(here, "tm", 2), r_here], axis=0)
     other = swap(mine, "tm", 1)
     return pl.pallas_call(
         assemble_kernel,
         in_specs=[SCALARS, VECTORS, VECTORS],
-        out_specs=pl.BlockSpec(memory_space=pltpu.HBM),
+        out_specs=VECTORS,
         out_shape=jax.ShapeDtypeStruct((2 * BEAMS, BEAMS), jnp.float32),
-        scratch_shapes=[pltpu.SemaphoreType.DMA((10,))],
         compiler_params=pltpu.CompilerParams(vmem_limit_bytes=PREPARE_VMEM),
         name="assemble",
     )(place, mine, other)

time: 76.6 us -> 75.5 us (0.986)
  waiting for transfers between devices: 21.5 us -> 20 us
  starting transfers between devices: 23.9 us -> 25 us
    ppermute x15 -> x16, waiting for transfers between devices: 21.1 us -> 19.5 us  [swap(): return lax.ppermute(value, axis, [(i, i ^ mask) for i in range(count)])]
    ppermute x15 -> x16, starting transfers between devices: 18.7 us -> 19.8 us  [swap(): return lax.ppermute(value, axis, [(i, i ^ mask) for i in range(count)])]
  transfers between devices with their start and end apart: 17 -> 18, of which waited for: 11 -> 10; matrix products, arithmetic and copies ran while one was open for 1% -> 1% of each run, Pallas kernels for 5% -> 5%
where the time goes in v3:
time: 75.5 us; the launch traced here: 75.4 us
  Pallas kernels  29.3 us (39%)
  starting transfers between devices  25 us (33%)
  waiting for transfers between devices  20 us (26%)
    ppermute x16, starting transfers between devices, swap(): return lax.ppermute(value, axis, [(i, i ^ mask) for i in range(count)])  19.8 us
    ppermute x16, waiting for transfers between devices, swap(): return lax.ppermute(value, axis, [(i, i ^ mask) for i in range(count)])  19.5 us
    pallas_call x1, Pallas kernels, referenced_gains(): pl.pallas_call(functools.partial(gains_kernel, channels=channels, interva...  13.7 us
    pallas_call x1, Pallas kernels, beam_products(): pl.pallas_call(functools.partial(calibrate_kernel, channels=channels, int...  10.6 us
    ppermute x1, starting transfers between devices, neighbour_gains(): lax.ppermute(jnp.where(odd, head, tail), 'tm', [(i, i ^ 1) for i in range...  4.38 us
    pallas_call x1, Pallas kernels, beam_products(): pl.pallas_call(own_products_kernel, in_specs=[SCALARS] + [VECTORS] * (2 +...  3.45 us
  transfers between devices with their start and end apart: 18, of which 10 were waited for; matrix products, arithmetic and copies ran while one was open for 1% of the time, Pallas kernels for 5%

profile of v3, /device:TPU:0, one launch (start us, length us, event | category | flops | bytes accessed | tf_op | source)
XLA Modules:
  0.0 75.4 jit_solution(17004819439080760922)
XLA Ops:
  0.0 13.7 %gains.1.mid_ref = f32[2,4,2,512]{3,2,1,0:T(2,128)S(1)} custom-call(bf16[2,4,2,512,512]{4,3,2,1,0:T(8,128)(2,1)} %vis_hbm.3, bf16[2,4,2,512,512]{4,3,2,1,0:T(8,128)(2,1)} %mod_hbm.1), custom_call_target="tpu_custom_call" | custom-call | flops 125829120 | bytes 16777216 | tf_op jit(solution)/shard_map/gains/pallas_call | solution.py:183
  13.8 0.8 %collective-permute-start.1 = (f32[2,2,2,512]{3,2,1,0:T(2,128)S(1)}, f32[2,2,2,512]{3,2,1,0:T(2,128)S(1)}, u32[]{:S(2)}, u32[]{:S(2)}) collective-permute-start(f32[2,2,2,512]{3,2,1,0:T(2,128)S(1)} %get-tuple-element.47), channel_id=1, source_target_pairs={{1,2},{2,1},{5,6},{6,5},{9,10},{10,9},{13,14},{14,13},{17,18},{18,... | collective-permute-start | bytes 49160 | tf_op jit(solution)/shard_map/ppermute | solution.py:528
  14.6 4.4 %collective-permute-start = (f32[2,2,2,512]{3,2,1,0:T(2,128)S(1)}, f32[2,2,2,512]{3,2,1,0:T(2,128)S(1)}, u32[]{:S(2)}, u32[]{:S(2)}) collective-permute-start(f32[2,2,2,512]{3,2,1,0:T(2,128)S(1)} %get-tuple-element.48), channel_id=1, source_target_pairs={{0,1},{1,0},{2,3},{3,2},{4,5},{5,4},{6,7},{7,6},{8,9},{9,8},{10,11... | collective-permute-start | bytes 49160 | tf_op jit(solution)/shard_map/ppermute | solution.py:526
  19.1 0.1 stack.56.place_ref
  19.2 0.2 prepare.1.table
  19.4 0.4 collective-permute-done
  19.9 10.6 %calibrate.1 = (f32[4,256,256]{2,1,0:T(8,128)S(1)}, f32[4,256,256]{2,1,0:T(8,128)S(1)}, f32[32,32,128]{2,1,0:T(8,128)S(1)}, f32[32,32,128]{2,1,0:T(8,128)S(1)}, ...) custom-call(s32[2,16]{1,0:T(2,128)S(1)} %copy-done.2, ...), custom_call_target="tpu_custom_call" | custom-call | flops 2000000000 | bytes 16777216 | tf_op jit(solution)/shard_map/calibrate/pallas_call | solution.py:406
  30.5 0.4 collective-permute-start.3
  30.9 3.4 %products.1 = (f32[4,256,256]{2,1,0:T(8,128)S(1)}, f32[4,256,256]{2,1,0:T(8,128)S(1)}) custom-call(s32[11]{0:T(128)S(1)} %stack.56.place_ref, bf16[8,256,128]{2,1,0:T(8,128)(2,1)S(1)} %copy-done, bf16[1024,256]{1,0:T(8,128)(2,1)S(1)} %prepare.1.table, f32[32,32,128]{2,1,0:T(8,128)S(1)} %get-tuple-element.23.refs_0_, ...), custom_call_target="tpu_custom_call" | custom-call | flops 2000000000 | bytes 2097152 | tf_op jit(solution)/shard_map/products/pallas_call | solution.py:432
  34.4 0.2 collective-permute-start.2
  34.6 1.6 %collective-permute-start.4 = (f32[4,96,256]{2,1,0:T(8,128)S(1)}, f32[4,96,256]{2,1,0:T(8,128)S(1)}, u32[]{:S(2)}, u32[]{:S(2)}) collective-permute-start(f32[4,96,256]{2,1,0:T(8,128)S(1)} %slice_add_fusion), channel_id=1, source_target_pairs={{0,4},{4,0},{8,12},{12,8},{16,20},{20,16},{24,28},{28,24},{1,5},{5... | collective-permute-start | bytes 1179656 | tf_op jit(solution)/shard_map/ppermute | solution.py:452
  36.2 0.8 %collective-permute-done.2 = f32[4,256,256]{2,1,0:T(8,128)S(1)} collective-permute-done((f32[4,256,256]{2,1,0:T(8,128)S(1)}, f32[4,256,256]{2,1,0:T(8,128)S(1)}, u32[]{:S(2)}, u32[]{:S(2)}) %collective-permute-start.2) | collective-permute-done | bytes 1048608 | tf_op jit(solution)/shard_map/ppermute | solution.py:452
  37.1 1.8 %collective-permute-start.9 = (f32[8,48,256]{2,1,0:T(8,128)S(1)}, f32[8,48,256]{2,1,0:T(8,128)S(1)}, u32[]{:S(2)}, u32[]{:S(2)}) collective-permute-start(f32[8,48,256]{2,1,0:T(8,128)S(1)} %pad_maximum_fusion), channel_id=1, source_target_pairs={{0,2},{1,3},{2,0},{3,1},{4,6},{5,7},{6,4},{7,5},{8,10},{9,11},{10,... | collective-permute-start | bytes 1179656 | tf_op jit(solution)/shard_map/ppermute | solution.py:452
  39.1 1.6 %collective-permute-start.8 = (f32[2,64,256]{2,1,0:T(8,128)S(1)}, f32[2,64,256]{2,1,0:T(8,128)S(1)}, u32[]{:S(2)}, u32[]{:S(2)}) collective-permute-start(f32[2,64,256]{2,1,0:T(8,128)S(1)} %get-tuple-element.39), channel_id=1, source_target_pairs={{0,8},{4,12},{8,0},{12,4},{16,24},{20,28},{24,16},{28,20},{1,9},{5... | collective-permute-start | bytes 393224 | tf_op jit(solution)/shard_map/ppermute | solution.py:452
  40.7 2.5 %collective-permute-start.6 = (f32[2,64,256]{2,1,0:T(8,128)S(1)}, f32[2,64,256]{2,1,0:T(8,128)S(1)}, u32[]{:S(2)}, u32[]{:S(2)}) collective-permute-start(f32[2,64,256]{2,1,0:T(8,128)S(1)} %get-tuple-element.40), channel_id=1, source_target_pairs={{0,24},{4,28},{8,16},{12,20},{16,8},{20,12},{24,0},{28,4},{1,25},{... | collective-permute-start | bytes 393224 | tf_op jit(solution)/shard_map/ppermute | solution.py:452
  43.2 0.1 collective-permute-start.7
  43.3 2.8 %collective-permute-done.4 = f32[4,96,256]{2,1,0:T(8,128)S(1)} collective-permute-done((f32[4,96,256]{2,1,0:T(8,128)S(1)}, f32[4,96,256]{2,1,0:T(8,128)S(1)}, u32[]{:S(2)}, u32[]{:S(2)}) %collective-permute-start.4) | collective-permute-done | bytes 393248 | tf_op jit(solution)/shard_map/ppermute | solution.py:452
  46.2 1.7 %collective-permute-start.5 = (f32[4,48,256]{2,1,0:T(8,128)S(1)}, f32[4,48,256]{2,1,0:T(8,128)S(1)}, u32[]{:S(2)}, u32[]{:S(2)}) collective-permute-start(f32[4,48,256]{2,1,0:T(8,128)S(1)} %slice.133), channel_id=1, source_target_pairs={{0,2},{1,3},{2,0},{3,1},{4,6},{5,7},{6,4},{7,5},{8,10},{9,11},{10,... | collective-permute-start | bytes 589832 | tf_op jit(solution)/shard_map/ppermute | solution.py:452
  47.9 0.9 %collective-permute-done.9 = f32[8,48,256]{2,1,0:T(8,128)S(1)} collective-permute-done((f32[8,48,256]{2,1,0:T(8,128)S(1)}, f32[8,48,256]{2,1,0:T(8,128)S(1)}, u32[]{:S(2)}, u32[]{:S(2)}) %collective-permute-start.9) | collective-permute-done | bytes 393248 | tf_op jit(solution)/shard_map/ppermute | solution.py:452
  48.8 1.6 %collective-permute-start.10 = (f32[4,48,256]{2,1,0:T(8,128)S(1)}, f32[4,48,256]{2,1,0:T(8,128)S(1)}, u32[]{:S(2)}, u32[]{:S(2)}) collective-permute-start(f32[4,48,256]{2,1,0:T(8,128)S(1)} %slice_add_fusion.4), channel_id=1, source_target_pairs={{0,4},{4,0},{8,12},{12,8},{16,20},{20,16},{24,28},{28,24},{1,5},{5... | collective-permute-start | bytes 589832 | tf_op jit(solution)/shard_map/ppermute | solution.py:452
  50.4 4.8 %collective-permute-done.7 = f32[2,64,256]{2,1,0:T(8,128)S(1)} collective-permute-done((f32[2,64,256]{2,1,0:T(8,128)S(1)}, f32[2,64,256]{2,1,0:T(8,128)S(1)}, u32[]{:S(2)}, u32[]{:S(2)}) %collective-permute-start.7) | collective-permute-done | bytes 131104 | tf_op jit(solution)/shard_map/ppermute | solution.py:452
  55.3 3.5 %collective-permute-start.11 = (f32[96,256]{1,0:T(8,128)S(1)}, f32[96,256]{1,0:T(8,128)S(1)}, u32[]{:S(2)}, u32[]{:S(2)}) collective-permute-start(f32[96,256]{1,0:T(8,128)S(1)} %get-tuple-element.42), channel_id=1, source_target_pairs={{0,24},{4,28},{8,16},{12,20},{16,8},{20,12},{24,0},{28,4},{1,25},{... | collective-permute-start | bytes 294920 | tf_op jit(solution)/shard_map/ppermute | solution.py:452
  58.8 0.9 %collective-permute-start.12 = (f32[96,256]{1,0:T(8,128)S(1)}, f32[96,256]{1,0:T(8,128)S(1)}, u32[]{:S(2)}, u32[]{:S(2)}) collective-permute-start(f32[96,256]{1,0:T(8,128)S(1)} %get-tuple-element.44), channel_id=1, source_target_pairs={{0,16},{4,20},{8,24},{12,28},{16,0},{20,4},{24,8},{28,12},{1,17},{... | collective-permute-start | bytes 294920 | tf_op jit(solution)/shard_map/ppermute | solution.py:452
  59.8 1.6 %collective-permute-start.15 = (f32[64,256]{1,0:T(8,128)S(1)}, f32[64,256]{1,0:T(8,128)S(1)}, u32[]{:S(2)}, u32[]{:S(2)}) collective-permute-start(f32[64,256]{1,0:T(8,128)S(1)} %slice_bitcast_fusion), channel_id=1, source_target_pairs={{0,4},{4,0},{8,12},{12,8},{16,20},{20,16},{24,28},{28,24},{1,5},{5... | collective-permute-start | bytes 196616 | tf_op jit(solution)/shard_map/ppermute | solution.py:452
  61.4 1.6 %collective-permute-done.11 = f32[96,256]{1,0:T(8,128)S(1)} collective-permute-done((f32[96,256]{1,0:T(8,128)S(1)}, f32[96,256]{1,0:T(8,128)S(1)}, u32[]{:S(2)}, u32[]{:S(2)}) %collective-permute-start.11) | collective-permute-done | bytes 98336 | tf_op jit(solution)/shard_map/ppermute | solution.py:452
  63.0 1.1 %collective-permute-done.13 = f32[96,256]{1,0:T(8,128)S(1)} collective-permute-done((f32[96,256]{1,0:T(8,128)S(1)}, f32[96,256]{1,0:T(8,128)S(1)}, u32[]{:S(2)}, u32[]{:S(2)}) %collective-permute-start.13) | collective-permute-done | bytes 98336 | tf_op jit(solution)/shard_map/ppermute | solution.py:452
  64.1 2.4 %collective-permute-done.12 = f32[96,256]{1,0:T(8,128)S(1)} collective-permute-done((f32[96,256]{1,0:T(8,128)S(1)}, f32[96,256]{1,0:T(8,128)S(1)}, u32[]{:S(2)}, u32[]{:S(2)}) %collective-permute-start.12) | collective-permute-done | bytes 98336 | tf_op jit(solution)/shard_map/ppermute | solution.py:452
  66.6 1.4 %collective-permute-start.14 = (f32[96,256]{1,0:T(8,128)S(1)}, f32[96,256]{1,0:T(8,128)S(1)}, u32[]{:S(2)}, u32[]{:S(2)}) collective-permute-start(f32[96,256]{1,0:T(8,128)S(1)} %fusion.20), channel_id=1, source_target_pairs={{0,2},{1,3},{2,0},{3,1},{4,6},{5,7},{6,4},{7,5},{8,10},{9,11},{10,... | collective-permute-start | bytes 294920 | tf_op jit(solution)/shard_map/ppermute | solution.py:452
  68.0 0.7 collective-permute-start.16
  68.7 3.6 %collective-permute-done.16 = f32[64,256]{1,0:T(8,128)S(1)} collective-permute-done((f32[64,256]{1,0:T(8,128)S(1)}, f32[64,256]{1,0:T(8,128)S(1)}, u32[]{:S(2)}, u32[]{:S(2)}) %collective-permute-start.16) | collective-permute-done | bytes 65568 | tf_op jit(solution)/shard_map/ppermute | solution.py:452
  72.5 1.5 %collective-permute-done.17.other = f32[256,256]{1,0:T(8,128)S(1)} collective-permute-done((f32[256,256]{1,0:T(8,128)S(1)}, f32[256,256]{1,0:T(8,128)S(1)}, u32[]{:S(2)}, u32[]{:S(2)}) %collective-permute-start.17) | collective-permute-done | bytes 262176 | tf_op jit(solution)/shard_map/ppermute | solution.py:452
  74.0 1.4 %assemble.1 = f32[512,256]{1,0:T(8,128)} custom-call(s32[11]{0:T(128)S(1)} %stack.56.place_ref, f32[256,256]{1,0:T(8,128)S(1)} %pad_maximum_fusion.1.mine, f32[256,256]{1,0:T(8,128)S(1)} %collective-permute-done.17.other), custom_call_target="tpu_custom_call" | custom-call | tf_op jit(solution)/shard_map/assemble/pallas_call | solution.py:503
  (42 shorter events, 0.8 us)
Async XLA Ops:
  0.0 19.0 %copy-start.4 = (s32[2,4,16]{2,1,0:T(4,128)S(1)}, s32[2,4,16]{2,1,0:T(4,128)}, u32[]{:S(2)}) copy-start(s32[2,4,16]{2,1,0:T(4,128)} %param.12) | copy-start | bytes 1540
  0.0 19.2 %copy-start.1 = (bf16[8,256,128]{2,1,0:T(8,128)(2,1)S(1)}, bf16[8,256,128]{2,1,0:T(8,128)(2,1)}, u32[]{:S(2)}) copy-start(bf16[8,256,128]{2,1,0:T(8,128)(2,1)} %right_ref) | copy-start | bytes 1572868
  0.0 19.9 %copy-start = (bf16[8,256,128]{2,1,0:T(8,128)(2,1)S(1)}, bf16[8,256,128]{2,1,0:T(8,128)(2,1)}, u32[]{:S(2)}) copy-start(bf16[8,256,128]{2,1,0:T(8,128)(2,1)} %left_ref.3) | copy-start | bytes 1572868
  0.0 19.9 %copy-start.2 = (s32[2,16]{1,0:T(2,128)S(1)}, s32[2,16]{1,0:T(2,128)}, u32[]{:S(2)}) copy-start(s32[2,16]{1,0:T(2,128)} %weight_ref.1) | copy-start | bytes 388
  0.0 19.9 %copy-start.3 = (s32[2]{0:T(128)S(1)}, s32[2]{0:T(128)}, u32[]{:S(2)}) copy-start(s32[2]{0:T(128)} %width_ref.1) | copy-start | bytes 28
  13.8 5.6 %collective-permute-start.1 = (f32[2,2,2,512]{3,2,1,0:T(2,128)S(1)}, f32[2,2,2,512]{3,2,1,0:T(2,128)S(1)}, u32[]{:S(2)}, u32[]{:S(2)}) collective-permute-start(f32[2,2,2,512]{3,2,1,0:T(2,128)S(1)} %get-tuple-element.47), channel_id=1, source_target_pairs={{1,2},{2,1},{5,6},{6,5},{9,10},{10,9},{13,14},{14,13},{17,18},{18,... | collective-permute-start | bytes 49160 | tf_op jit(solution)/shard_map/ppermute | solution.py:528
  14.6 5.2 %collective-permute-start = (f32[2,2,2,512]{3,2,1,0:T(2,128)S(1)}, f32[2,2,2,512]{3,2,1,0:T(2,128)S(1)}, u32[]{:S(2)}, u32[]{:S(2)}) collective-permute-start(f32[2,2,2,512]{3,2,1,0:T(2,128)S(1)} %get-tuple-element.48), channel_id=1, source_target_pairs={{0,1},{1,0},{2,3},{3,2},{4,5},{5,4},{6,7},{7,6},{8,9},{9,8},{10,11... | collective-permute-start | bytes 49160 | tf_op jit(solution)/shard_map/ppermute | solution.py:526
  30.5 4.1 %collective-permute-start.3 = (f32[4,256,256]{2,1,0:T(8,128)S(1)}, f32[4,256,256]{2,1,0:T(8,128)S(1)}, u32[]{:S(2)}, u32[]{:S(2)}) collective-permute-start(f32[4,256,256]{2,1,0:T(8,128)S(1)} %get-tuple-element.34), channel_id=1, source_target_pairs={{0,1},{1,0},{2,3},{3,2},{4,5},{5,4},{6,7},{7,6},{8,9},{9,8},{10,11... | collective-permute-start | bytes 3145736 | tf_op jit(solution)/shard_map/ppermute | solution.py:452
  34.4 2.7 %collective-permute-start.2 = (f32[4,256,256]{2,1,0:T(8,128)S(1)}, f32[4,256,256]{2,1,0:T(8,128)S(1)}, u32[]{:S(2)}, u32[]{:S(2)}) collective-permute-start(f32[4,256,256]{2,1,0:T(8,128)S(1)} %get-tuple-element.32), channel_id=1, source_target_pairs={{0,1},{1,0},{2,3},{3,2},{4,5},{5,4},{6,7},{7,6},{8,9},{9,8},{10,11... | collective-permute-start | bytes 3145736 | tf_op jit(solution)/shard_map/ppermute | solution.py:452
  34.6 11.4 %collective-permute-start.4 = (f32[4,96,256]{2,1,0:T(8,128)S(1)}, f32[4,96,256]{2,1,0:T(8,128)S(1)}, u32[]{:S(2)}, u32[]{:S(2)}) collective-permute-start(f32[4,96,256]{2,1,0:T(8,128)S(1)} %slice_add_fusion), channel_id=1, source_target_pairs={{0,4},{4,0},{8,12},{12,8},{16,20},{20,16},{24,28},{28,24},{1,5},{5... | collective-permute-start | bytes 1179656 | tf_op jit(solution)/shard_map/ppermute | solution.py:452
  37.1 11.6 %collective-permute-start.9 = (f32[8,48,256]{2,1,0:T(8,128)S(1)}, f32[8,48,256]{2,1,0:T(8,128)S(1)}, u32[]{:S(2)}, u32[]{:S(2)}) collective-permute-start(f32[8,48,256]{2,1,0:T(8,128)S(1)} %pad_maximum_fusion), channel_id=1, source_target_pairs={{0,2},{1,3},{2,0},{3,1},{4,6},{5,7},{6,4},{7,5},{8,10},{9,11},{10,... | collective-permute-start | bytes 1179656 | tf_op jit(solution)/shard_map/ppermute | solution.py:452
  39.1 11.3 %collective-permute-start.8 = (f32[2,64,256]{2,1,0:T(8,128)S(1)}, f32[2,64,256]{2,1,0:T(8,128)S(1)}, u32[]{:S(2)}, u32[]{:S(2)}) collective-permute-start(f32[2,64,256]{2,1,0:T(8,128)S(1)} %get-tuple-element.39), channel_id=1, source_target_pairs={{0,8},{4,12},{8,0},{12,4},{16,24},{20,28},{24,16},{28,20},{1,9},{5... | collective-permute-start | bytes 393224 | tf_op jit(solution)/shard_map/ppermute | solution.py:452
  40.7 9.7 %collective-permute-start.6 = (f32[2,64,256]{2,1,0:T(8,128)S(1)}, f32[2,64,256]{2,1,0:T(8,128)S(1)}, u32[]{:S(2)}, u32[]{:S(2)}) collective-permute-start(f32[2,64,256]{2,1,0:T(8,128)S(1)} %get-tuple-element.40), channel_id=1, source_target_pairs={{0,24},{4,28},{8,16},{12,20},{16,8},{20,12},{24,0},{28,4},{1,25},{... | collective-permute-start | bytes 393224 | tf_op jit(solution)/shard_map/ppermute | solution.py:452
  43.2 12.0 %collective-permute-start.7 = (f32[2,64,256]{2,1,0:T(8,128)S(1)}, f32[2,64,256]{2,1,0:T(8,128)S(1)}, u32[]{:S(2)}, u32[]{:S(2)}) collective-permute-start(f32[2,64,256]{2,1,0:T(8,128)S(1)} %get-tuple-element.41), channel_id=1, source_target_pairs={{0,16},{4,20},{8,24},{12,28},{16,0},{20,4},{24,8},{28,12},{1,17},{... | collective-permute-start | bytes 393224 | tf_op jit(solution)/shard_map/ppermute | solution.py:452
  46.2 9.0 %collective-permute-start.5 = (f32[4,48,256]{2,1,0:T(8,128)S(1)}, f32[4,48,256]{2,1,0:T(8,128)S(1)}, u32[]{:S(2)}, u32[]{:S(2)}) collective-permute-start(f32[4,48,256]{2,1,0:T(8,128)S(1)} %slice.133), channel_id=1, source_target_pairs={{0,2},{1,3},{2,0},{3,1},{4,6},{5,7},{6,4},{7,5},{8,10},{9,11},{10,... | collective-permute-start | bytes 589832 | tf_op jit(solution)/shard_map/ppermute | solution.py:452
  48.8 6.4 %collective-permute-start.10 = (f32[4,48,256]{2,1,0:T(8,128)S(1)}, f32[4,48,256]{2,1,0:T(8,128)S(1)}, u32[]{:S(2)}, u32[]{:S(2)}) collective-permute-start(f32[4,48,256]{2,1,0:T(8,128)S(1)} %slice_add_fusion.4), channel_id=1, source_target_pairs={{0,4},{4,0},{8,12},{12,8},{16,20},{20,16},{24,28},{28,24},{1,5},{5... | collective-permute-start | bytes 589832 | tf_op jit(solution)/shard_map/ppermute | solution.py:452
  55.3 7.7 %collective-permute-start.11 = (f32[96,256]{1,0:T(8,128)S(1)}, f32[96,256]{1,0:T(8,128)S(1)}, u32[]{:S(2)}, u32[]{:S(2)}) collective-permute-start(f32[96,256]{1,0:T(8,128)S(1)} %get-tuple-element.42), channel_id=1, source_target_pairs={{0,24},{4,28},{8,16},{12,20},{16,8},{20,12},{24,0},{28,4},{1,25},{... | collective-permute-start | bytes 294920 | tf_op jit(solution)/shard_map/ppermute | solution.py:452
  58.8 5.3 %collective-permute-start.13 = (f32[96,256]{1,0:T(8,128)S(1)}, f32[96,256]{1,0:T(8,128)S(1)}, u32[]{:S(2)}, u32[]{:S(2)}) collective-permute-start(f32[96,256]{1,0:T(8,128)S(1)} %get-tuple-element.43), channel_id=1, source_target_pairs={{0,8},{4,12},{8,0},{12,4},{16,24},{20,28},{24,16},{28,20},{1,9},{5... | collective-permute-start | bytes 294920 | tf_op jit(solution)/shard_map/ppermute | solution.py:452
  58.8 7.7 %collective-permute-start.12 = (f32[96,256]{1,0:T(8,128)S(1)}, f32[96,256]{1,0:T(8,128)S(1)}, u32[]{:S(2)}, u32[]{:S(2)}) collective-permute-start(f32[96,256]{1,0:T(8,128)S(1)} %get-tuple-element.44), channel_id=1, source_target_pairs={{0,16},{4,20},{8,24},{12,28},{16,0},{20,4},{24,8},{28,12},{1,17},{... | collective-permute-start | bytes 294920 | tf_op jit(solution)/shard_map/ppermute | solution.py:452
  59.8 8.2 %collective-permute-start.15 = (f32[64,256]{1,0:T(8,128)S(1)}, f32[64,256]{1,0:T(8,128)S(1)}, u32[]{:S(2)}, u32[]{:S(2)}) collective-permute-start(f32[64,256]{1,0:T(8,128)S(1)} %slice_bitcast_fusion), channel_id=1, source_target_pairs={{0,4},{4,0},{8,12},{12,8},{16,20},{20,16},{24,28},{28,24},{1,5},{5... | collective-permute-start | bytes 196616 | tf_op jit(solution)/shard_map/ppermute | solution.py:452
  66.6 5.8 %collective-permute-start.14 = (f32[96,256]{1,0:T(8,128)S(1)}, f32[96,256]{1,0:T(8,128)S(1)}, u32[]{:S(2)}, u32[]{:S(2)}) collective-permute-start(f32[96,256]{1,0:T(8,128)S(1)} %fusion.20), channel_id=1, source_target_pairs={{0,2},{1,3},{2,0},{3,1},{4,6},{5,7},{6,4},{7,5},{8,10},{9,11},{10,... | collective-permute-start | bytes 294920 | tf_op jit(solution)/shard_map/ppermute | solution.py:452
  68.0 4.3 %collective-permute-start.16 = (f32[64,256]{1,0:T(8,128)S(1)}, f32[64,256]{1,0:T(8,128)S(1)}, u32[]{:S(2)}, u32[]{:S(2)}) collective-permute-start(f32[64,256]{1,0:T(8,128)S(1)} %fusion.24), channel_id=1, source_target_pairs={{0,2},{1,3},{2,0},{3,1},{4,6},{5,7},{6,4},{7,5},{8,10},{9,11},{10,... | collective-permute-start | bytes 196616 | tf_op jit(solution)/shard_map/ppermute | solution.py:452
  72.4 1.6 %collective-permute-start.17 = (f32[256,256]{1,0:T(8,128)S(1)}, f32[256,256]{1,0:T(8,128)S(1)}, u32[]{:S(2)}, u32[]{:S(2)}) collective-permute-start(f32[256,256]{1,0:T(8,128)S(1)} %pad_maximum_fusion.1.mine), channel_id=1, source_target_pairs={{0,1},{1,0},{2,3},{3,2},{4,5},{5,4},{6,7},{7,6},{8,9},{9,8},{10,11... | collective-permute-start | bytes 786440 | tf_op jit(solution)/shard_map/ppermute | solution.py:452
